TPU v7x, 256 devices: a whole 4x4x8 slice. The times are simulated.
256 devices in a mesh: dap: 64 (over x, z, y_hi), head: 4 (over y_lo, core).
Axes of the slice: x: 4, y: 4 (y_hi: 2, y_lo: 2; y = y_hi * 2 + y_lo), z: 8, core: 2. Of those that a mesh axis runs over, the one named last changes fastest.
Arguments:
- pair: bfloat16 [1024, 1024, 128], P('dap'), may hold values from -600 to 600
- residue_mask: int32 [1024], replicated, may hold values 0 or 1
- chain_breaks: int32 [1024], replicated, may hold values 0 or 1
- w_query: bfloat16 [128, 128], P(None, 'head'), may hold values from -0.5 to 0.5
- w_key: bfloat16 [128, 128], P(None, 'head'), may hold values from -0.5 to 0.5
- w_value: bfloat16 [128, 128], P(None, 'head'), may hold values from -0.5 to 0.5
- w_gate: bfloat16 [128, 128], P(None, 'head'), may hold values from -0.5 to 0.5
- w_bias: bfloat16 [128, 4], P(None, 'head'), may hold values from -29 to 29
- w_out: bfloat16 [128, 128], P('head'), may hold values from -0.5 to 0.5
Outputs:
- update: bfloat16 [1024, 1024, 128], P('dap', None, 'head')
All inputs are finite; a program needn't handle non-finite values.
Results may differ from a plain program's by a relative error of at most 0.019.
Values may be sent and summed in bfloat16 or wider, within the bound.
No kernel may reach another device: no remote copies, remote signals or barrier semaphores. Data moves between devices by JAX's collectives and lax.ppermute only.
A program may use at most 64 MiB of HBM per device.

v0:
```python
import functools
import math

import jax
import jax.numpy as jnp
from jax import lax
from jax.experimental import pallas as pl
from jax.experimental.pallas import tpu as pltpu
from jax.sharding import PartitionSpec as P

bf16 = jnp.bfloat16
f32 = jnp.float32

N = 1024
C = 128
HEADS = 4
WIDTH = 32
NX, NZ, NY = 4, 8, 2
DAP = NX * NZ * NY
ROWS = N // DAP
COLS = N // (DAP * HEADS)
TILE = 512
LOG2E = math.log2(math.e)
PENALTY = -2.0
MASKED = -1e9
NT = (((1,), (1,)), ((), ()))
TN = (((0,), (0,)), ((), ()))


def dot(a, b, dims=(((1,), (0,)), ((), ()))):
    return lax.dot_general(a, b, dims, preferred_element_type=f32)


def norm_kernel(head_ref, pair_ref, normed_ref, send_ref):
    average = jnp.full((C, C), 1.0 / C, bf16)
    twice = jnp.full((2 * C, C), 1.0 / C, bf16)
    for r in range(pair_ref.shape[0]):
        x = pair_ref[r]
        centered = x.astype(f32) - dot(x, average)
        square = centered * centered
        high = square.astype(bf16)
        low = (square - high.astype(f32)).astype(bf16)
        variance = dot(jnp.concatenate([high, low], 1), twice)
        normed_ref[r] = (centered * lax.rsqrt(variance + 1e-05)).astype(bf16)
        for c in range(COLS):
            start = pl.multiple_of(c * HEADS * DAP + head_ref[0] * DAP, DAP)
            send_ref[c, r] = normed_ref[r, pl.ds(start, DAP), :]


def norm_call(pair, head):
    step = 4
    return pl.pallas_call(
        norm_kernel,
        grid_spec=pltpu.PrefetchScalarGridSpec(
            num_scalar_prefetch=1,
            grid=(ROWS // step,),
            in_specs=[pl.BlockSpec((step, N, C), lambda r, h: (r, 0, 0))],
            out_specs=[
                pl.BlockSpec((step, N, C), lambda r, h: (r, 0, 0)),
                pl.BlockSpec((COLS, step, DAP, C), lambda r, h: (0, r, 0, 0)),
            ],
        ),
        out_shape=[
            jax.ShapeDtypeStruct((ROWS, N, C), bf16),
            jax.ShapeDtypeStruct((COLS, ROWS, DAP, C), bf16),
        ],
        cost_estimate=cost(6, 9 * 2**20),
        compiler_params=pltpu.CompilerParams(vmem_limit_bytes=32 * 2**20),
        name="norm",
    )(head, pair)


def cost(us, moved=0):
    return pl.CostEstimate(flops=int(us * 1.1e9), bytes_accessed=moved, transcendentals=0)


def bias_kernel(normed_ref, w_ref, out_ref):
    rows = normed_ref.shape[0]
    for r in range(rows):
        b = dot(w_ref[...], normed_ref[r], NT)
        out_ref[0, pl.ds(r, 1), :] = b[0:1].astype(bf16)
        out_ref[1, pl.ds(r, 1), :] = b[1:2].astype(bf16)


def bias_call(normed, w_two):
    return pl.pallas_call(
        bias_kernel,
        in_specs=[pl.BlockSpec(memory_space=pltpu.VMEM)] * 2,
        out_specs=pl.BlockSpec(memory_space=pltpu.VMEM),
        out_shape=jax.ShapeDtypeStruct((2, ROWS, N), bf16),
        cost_estimate=cost(1.5),
        compiler_params=pltpu.CompilerParams(vmem_limit_bytes=32 * 2**20),
        name="bias",
    )(normed, w_two)


def pack_kernel(wq, wk, wv, wg, wo, out_ref):
    for n, ref in enumerate((wq, wk, wv, wg, wo)):
        out_ref[n] = ref[...]


def pack_call(*weights):
    return pl.pallas_call(
        pack_kernel,
        in_specs=[pl.BlockSpec(memory_space=pltpu.VMEM)] * 5,
        out_specs=pl.BlockSpec(memory_space=pltpu.VMEM),
        out_shape=jax.ShapeDtypeStruct((5, WIDTH, C), bf16),
        cost_estimate=cost(1),
        name="pack",
    )(*weights)


def mask_kernel(place_ref, mask_ref, breaks_ref, extra_ref, keep_ref):
    chunk = N // NX
    row = breaks_ref[0:1, :].astype(f32)
    ones = jnp.ones((C, N), f32)
    breaks = (ones * row).astype(bf16)
    mask = (ones * (mask_ref[0:1, :] > 0).astype(f32)).astype(bf16)
    before = (
        lax.broadcasted_iota(jnp.int32, (N, N), 0) <= lax.broadcasted_iota(jnp.int32, (N, N), 1)
    )
    chain_row = dot(breaks[:16], jnp.where(before, 1.0, 0.0).astype(bf16))[0:1]
    for s in range(NX):
        k = jnp.concatenate(
            [
                lax.broadcasted_iota(jnp.int32, (ROWS, N), 0) + dap_of(place_ref, s, n, t) * ROWS
                for n in range(NZ) for t in range(NY)
            ],
            0,
        )
        j = lax.broadcasted_iota(jnp.int32, (chunk, N), 1)
        chain = dot(jnp.where(j <= k, 1.0, 0.0).astype(bf16), breaks, NT)
        keep = dot(jnp.where(j == k, 1.0, 0.0).astype(bf16), mask, NT)
        keep_ref[s] = keep.astype(bf16)
        for t in range(N // C):
            at = slice(t * C, (t + 1) * C)
            value = jnp.where(chain == chain_row[:, at], 0.0, PENALTY)
            extra_ref[s, :, at] = jnp.where(keep > 0.5, value, MASKED).astype(bf16)


def mask_call(place, mask, breaks):
    return pl.pallas_call(
        mask_kernel,
        in_specs=[pl.BlockSpec(memory_space=pltpu.SMEM)] + [pl.BlockSpec(memory_space=pltpu.VMEM)] * 2,
        out_specs=[pl.BlockSpec(memory_space=pltpu.VMEM)] * 2,
        out_shape=[
            jax.ShapeDtypeStruct((NX, N // NX, N), bf16),
            jax.ShapeDtypeStruct((NX, N // NX, C), bf16),
        ],
        cost_estimate=cost(2),
        compiler_params=pltpu.CompilerParams(vmem_limit_bytes=32 * 2**20),
        name="mask",
    )(place, mask, breaks)


def order_weights(upper_ref, parts, w_ref, spread_ref):
    for h in range(HEADS):
        low, high = parts[h // 2 * 2], parts[h // 2 * 2 + 1]
        w_ref[h] = jnp.where(upper_ref[0] == h % 2, low[...], high[...])
    w_out = jnp.concatenate([w_ref[h, 4] for h in range(HEADS)], 0)
    a = lax.broadcasted_iota(jnp.int32, (C, C), 0)
    b = lax.broadcasted_iota(jnp.int32, (C, C), 1)
    for o in range(HEADS):
        for c in range(COLS):
            pick = (b // WIDTH == c) & (a == b - c * WIDTH + o * WIDTH)
            moved = dot(w_out, jnp.where(pick, 1.0, 0.0).astype(bf16))
            spread_ref[o, c * C : (c + 1) * C] = moved.astype(bf16)


AROUND = (0, -1, 1, -2, 2, -3, 3, 4)


def dap_of(place_ref, s, n, t):
    x, z, y = place_ref[0], place_ref[1], place_ref[2]
    return ((x + s) & (NX - 1)) * (NZ * NY) + ((z + NZ + AROUND[n]) & (NZ - 1)) * NY + (y ^ t)


def project(c, place_ref, recv_ref, keep_ref, w_ref, k_ref, q_ref, v_ref, g_ref):
    chunk = N // NX
    weight = lambda n: w_ref[:, n].reshape(C, C)
    whole = recv_ref[:, c].reshape(N, C)
    q = (dot(weight(0), whole, NT) * WIDTH ** (-0.5)).astype(bf16)
    q = q.astype(f32) * LOG2E
    high = q.astype(bf16)
    low = (q - high.astype(f32)).astype(bf16)
    for h in range(HEADS):
        rows = slice(h * WIDTH, (h + 1) * WIDTH)
        q_ref[c, h, 0:WIDTH] = high[rows]
        q_ref[c, h, WIDTH : 2 * WIDTH] = low[rows]
    g_ref[c] = jax.nn.sigmoid(dot(weight(3), whole, NT)).astype(bf16)
    ones = jnp.where(lax.broadcasted_iota(jnp.int32, (16, chunk), 0) == 0, 1.0, 0.0).astype(bf16)
    for s in range(NX):
        rows = jnp.concatenate(
            [recv_ref[dap_of(place_ref, s, n, t), c] for n in range(NZ) for t in range(NY)], 0
        )
        here = slice(s * chunk, (s + 1) * chunk)
        for p in range(2):
            first, second = w_ref[2 * p, 1], w_ref[2 * p + 1, 1]
            wk = jnp.concatenate([first, first, second, second], 0)
            k_ref[c, p, here] = dot(rows, wk, NT).astype(bf16) * keep_ref[s]
        v = dot(weight(2), rows, NT).astype(bf16)
        for h in range(HEADS):
            v_ref[c, h, 0:WIDTH, here] = v[h * WIDTH : (h + 1) * WIDTH]
            v_ref[c, h, WIDTH : WIDTH + 16, here] = ones


def attend_kernel(
    place_ref, upper_ref, recv_ref, keep_ref, extra_ref, *rest
):
    parts, bias_refs = rest[:4], rest[4:24]
    out_ref, w_ref, wout_ref, k_ref, q_ref, v_ref, g_ref, comb, s_scr, gated = rest[24:]
    lanes = pl.ds(pl.multiple_of(pl.program_id(0) * TILE, TILE), TILE)

    @pl.when(pl.program_id(0) == 0)
    def _():
        order_weights(upper_ref, parts, w_ref, wout_ref)

        def step(c, carry):
            project(c, place_ref, recv_ref, keep_ref, w_ref, k_ref, q_ref, v_ref, g_ref)
            return carry

        lax.fori_loop(0, COLS, step, 0)

    chunk = N // NX
    zeros = jnp.zeros((2 * WIDTH, TILE), bf16)

    def bias(h, s):
        parts = bias_refs[10 * (h // 2) : 10 * (h // 2) + 10]
        if s == 2:
            return [parts[2 + 5 * group + h % 2][0] for group in range(2)]
        return [parts[(0, 1, None, 4)[s] + 5 * group][h % 2] for group in range(2)]

    def score(h, c, s, q, top):
        k = k_ref[c, h // 2, s * chunk : (s + 1) * chunk]
        scores = dot(k, q) + comb[h % 2, s]
        s_scr[c % 2, s] = scores
        high = jnp.max(scores.reshape(chunk // 8, 8, TILE), 0)
        return high if top is None else jnp.maximum(top, high)

    def weigh(h, c, s, top, total):
        weights = jnp.exp2(s_scr[c % 2, s] - top).astype(bf16)
        part = dot(v_ref[c, h, :, s * chunk : (s + 1) * chunk], weights)
        return part if total is None else total + part

    def finish(h, c, total):
        attended = (total[0:WIDTH] / total[WIDTH : WIDTH + 1]).astype(bf16).astype(f32)
        rows = slice(h * WIDTH, (h + 1) * WIDTH)
        gated[c, rows] = (g_ref[c, rows, lanes].astype(f32) * attended).astype(bf16)

    steps = [(h, c) for h in range(HEADS) for c in range(COLS)]
    before = None
    for h, c in steps + [(None, None)]:
        if h is not None:
            if c == 0:
                for s in range(NX):
                    start = 0
                    for part in bias(h, s):
                        here = slice(start, start + part.shape[0])
                        extra = extra_ref[s, here].astype(f32)
                        value = jnp.where(extra > 0.5 * MASKED, part.astype(f32) + extra, MASKED)
                        comb[h % 2, s, here] = value * LOG2E
                        start += part.shape[0]
            q = q_ref[c, h, :, lanes]
            q = jnp.concatenate([q, zeros] if h % 2 == 0 else [zeros, q], 0)
        top = total = None
        for s in range(NX):
            if h is not None:
                top = score(h, c, s, q, top)
            if before is not None:
                total = weigh(before[0], before[1], s, before[2], total)
        if before is not None:
            finish(before[0], before[1], total)
        if h is not None:
            before = (h, c, jnp.max(top, 0, keepdims=True))
    joined = gated[...].reshape(COLS * C, TILE)
    for o in range(HEADS):
        out_ref[o] = dot(joined, wout_ref[o], TN).astype(bf16)


def attend_call(place, upper, recv, keep, extra, parts, pieces):
    whole = lambda shape: pl.BlockSpec(shape, lambda t: (0,) * len(shape))
    along = lambda shape: pl.BlockSpec(shape, lambda t: (0,) * (len(shape) - 1) + (t,))
    return pl.pallas_call(
        attend_kernel,
        grid=(N // TILE,),
        in_specs=[
            pl.BlockSpec(memory_space=pltpu.SMEM),
            pl.BlockSpec(memory_space=pltpu.SMEM),
            whole((DAP, COLS, ROWS, C)),
            whole((NX, N // NX, C)),
            along((NX, N // NX, TILE)),
        ]
        + [whole((5, WIDTH, C))] * 4
        + [along(piece.shape[:2] + (TILE,)) for piece in pieces],
        out_specs=pl.BlockSpec((HEADS, TILE, C), lambda t: (0, t, 0)),
        scratch_shapes=[
            pltpu.VMEM((HEADS, 5, WIDTH, C), bf16),
            pltpu.VMEM((HEADS, COLS * C, C), bf16),
            pltpu.VMEM((COLS, 2, N, C), bf16),
            pltpu.VMEM((COLS, HEADS, 2 * WIDTH, N), bf16),
            pltpu.VMEM((COLS, HEADS, WIDTH + 16, N), bf16),
            pltpu.VMEM((COLS, C, N), bf16),
            pltpu.VMEM((2, NX, N // NX, TILE), f32),
            pltpu.VMEM((2, NX, N // NX, TILE), f32),
            pltpu.VMEM((COLS, C, TILE), bf16),
        ],
        out_shape=jax.ShapeDtypeStruct((HEADS, N, C), bf16),
        cost_estimate=cost(40),
        compiler_params=pltpu.CompilerParams(vmem_limit_bytes=60 * 2**20),
        name="attend",
    )(place, upper, recv, keep, extra, *parts, *pieces)


def at(x, z, y, head):
    return (((x % NX) * NZ + z % NZ) * NY + y % NY) * HEADS + head


def send(value, dx, dz, dy=0):
    pairs = [
        (at(x, z, y, head), at(x + dx, z + dz, y + dy, head ^ (2 * dy)))
        for x in range(NX) for z in range(NZ) for y in range(NY) for head in range(HEADS)
    ]
    return lax.ppermute(value, ("dap", "head"), pairs)


def gather_bias(rows, out):
    beside = send(rows, 0, 0, 1)
    up = jnp.concatenate([send(rows, 0, 1), send(rows, 0, 1, 1)], 1)
    down = jnp.concatenate([send(rows, 0, -1), send(rows, 0, -1, 1)], 1)
    near = jnp.concatenate([rows, beside, up, down], 1)
    got = []
    for step in range(2, 4):
        up, down = send(up, 0, 1), send(down, 0, -1)
        got += [up, down]
    last = [send(up[:1], 0, 1), send(down[1:], 0, -1)]
    out, *last = lax.optimization_barrier((out, *last))
    last = jnp.concatenate(last, 0)
    far = jnp.concatenate(got + [last], 1)
    own = []
    for group in (near, far):
        left, right = send(group, 1, 0), send(group, -1, 0)
        own += [group, right, send(left[:1], 1, 0), send(right[1:], -1, 0), left]
    swap = [(h, h ^ 1) for h in range(HEADS)]
    return own + [lax.ppermute(piece, "head", swap) for piece in own], out


def body(pair, residue_mask, chain_breaks, w_query, w_key, w_value, w_gate, w_bias, w_out):
    dap = lax.axis_index("dap").astype(jnp.int32)
    head = lax.axis_index("head").astype(jnp.int32)
    place = jnp.stack([dap // (NZ * NY), (dap // NY) & (NZ - 1), dap & (NY - 1)])
    w_own = w_bias.T
    w_other = lax.ppermute(w_own, "head", [(h, h ^ 2) for h in range(HEADS)])
    upper = head >= 2
    w_two = jnp.concatenate(
        [jnp.where(upper, w_other, w_own), jnp.where(upper, w_own, w_other), jnp.zeros((14, C), bf16)], 0
    )
    mine = pack_call(w_query.T, w_key.T, w_value.T, w_gate.T, w_out)
    parts = [mine] + [lax.ppermute(mine, "head", [(h, h ^ n) for h in range(HEADS)]) for n in (2, 1, 3)]
    wide = lambda v: jnp.broadcast_to(v[None], (8, N))
    extra, keep = mask_call(place, wide(residue_mask), wide(chain_breaks))
    which, extra, keep = lax.optimization_barrier((head[None], extra, keep))
    normed, out = norm_call(pair, which)
    pieces, out = gather_bias(bias_call(normed, w_two), jnp.transpose(out, (2, 0, 1, 3)))
    recv = lax.all_to_all(out, "dap", 0, 0, tiled=True)
    update = attend_call(place, (head >> 1)[None], recv, keep, extra, parts, pieces)
    update = update.reshape(HEADS * DAP, ROWS, C)
    update = lax.all_to_all(update, ("head", "dap"), 0, 0, tiled=True)
    update = update.reshape(HEADS * DAP, ROWS, COLS, WIDTH)
    return jnp.transpose(update, (1, 2, 0, 3)).reshape(ROWS, N, WIDTH)


def solution(mesh):
    placed = (
        P("dap", None, None), P(), P(),
        P(None, "head"), P(None, "head"), P(None, "head"), P(None, "head"), P(None, "head"),
        P("head", None),
    )
    return jax.shard_map(
        body, mesh=mesh, in_specs=placed, out_specs=P("dap", None, "head"), check_vma=False
    )
```

profile of v0, /device:TPU:1, one launch (start us, length us, event | category | flops | bytes accessed | tf_op | source)
XLA Modules:
  0.0 190.0 jit_solution(11683913957947206146)
XLA Ops:
  0.0 2.1 %collective-permute-start = (bf16[1,128]{1,0:T(2,128)(2,1)}, bf16[1,128]{1,0:T(2,128)(2,1)S(1)}, u32[]{:S(2)}, u32[]{:S(2)}) collective-permute-start(bf16[1,128]{1,0:T(2,128)(2,1)} %bitcast.23), channel_id=1, source_target_pairs={{0,2},{1,3},{2,0},{3,1},{4,6},{5,7},{6,4},{7,5},{8,10},{9,11},{10,... | collective-permute-start | bytes 776 | tf_op jit(solution)/shard_map/ppermute | solution.py:352
  4.0 2.4 %mask.1 = (bf16[4,256,1024]{2,1,0:T(8,128)(2,1)S(1)}, bf16[4,256,128]{2,1,0:T(8,128)(2,1)S(1)}) custom-call(s32[3]{0:T(128)S(1)} %pad_add_fusion.place_ref, s32[8,1024]{1,0:T(8,128)S(1)} %broadcast_in_dim.23.mask_ref, s32[8,1024]{1,0:T(8,128)S(1)} %broadcast_in_dim.24.breaks_ref), custom_call_target="tpu_custom_call" | custom-call | flops 2200000000 | tf_op jit(solution)/shard_map/mask/pallas_call | solution.py:142
  6.4 4.6 %norm.1 = (bf16[16,1024,128]{2,1,0:T(8,128)(2,1)S(1)}, bf16[4,16,64,128]{3,2,1,0:T(8,128)(2,1)S(1)}) custom-call(s32[1]{0:T(128)} %bitcast.4.head_ref, bf16[16,1024,128]{2,1,0:T(8,128)(2,1)S(1)} %copy-done.1), custom_call_target="tpu_custom_call" | custom-call | flops 6600000000 | bytes 9437184 | tf_op jit(solution)/shard_map/norm/pallas_call | solution.py:52
  11.0 1.6 copy.22
  14.0 2.0 %collective-permute-start.14 = (bf16[2,16,1024]{2,1,0:T(8,128)(2,1)S(1)}, bf16[2,16,1024]{2,1,0:T(8,128)(2,1)S(1)}, u32[]{:S(2)}, u32[]{:S(2)}) collective-permute-start(bf16[2,16,1024]{2,1,0:T(8,128)(2,1)S(1)} %bias.1), channel_id=1, source_target_pairs={{0,6},{1,7},{2,4},{3,5},{4,2},{5,3},{6,0},{7,1},{8,14},{9,15},{10,... | collective-permute-start | bytes 196616 | tf_op jit(solution)/shard_map/ppermute | solution.py:323
  16.0 6.1 %collective-permute-start.7 = (bf16[2,16,1024]{2,1,0:T(8,128)(2,1)S(1)}, bf16[2,16,1024]{2,1,0:T(8,128)(2,1)S(1)}, u32[]{:S(2)}, u32[]{:S(2)}) collective-permute-start(bf16[2,16,1024]{2,1,0:T(8,128)(2,1)S(1)} %bias.1), channel_id=1, source_target_pairs={{0,62},{1,63},{2,60},{3,61},{4,58},{5,59},{6,56},{7,57},{8,6},{9,7... | collective-permute-start | bytes 196616 | tf_op jit(solution)/shard_map/ppermute | solution.py:323
  22.8 2.4 %collective-permute-start.2 = (bf16[2,16,1024]{2,1,0:T(8,128)(2,1)S(1)}, bf16[2,16,1024]{2,1,0:T(8,128)(2,1)S(1)}, u32[]{:S(2)}, u32[]{:S(2)}) collective-permute-start(bf16[2,16,1024]{2,1,0:T(8,128)(2,1)S(1)} %bias.1), channel_id=1, source_target_pairs={{0,14},{1,15},{2,12},{3,13},{4,10},{5,11},{6,8},{7,9},{8,22},{9,23... | collective-permute-start | bytes 196616 | tf_op jit(solution)/shard_map/ppermute | solution.py:323
  25.8 2.7 %collective-permute-start.8 = (bf16[2,32,1024]{2,1,0:T(8,128)(2,1)S(1)}, bf16[2,32,1024]{2,1,0:T(8,128)(2,1)S(1)}, u32[]{:S(2)}, u32[]{:S(2)}) collective-permute-start(bf16[2,32,1024]{2,1,0:T(8,128)(2,1)S(1)} %pad_maximum_fusion.1), channel_id=1, source_target_pairs={{0,56},{1,57},{2,58},{3,59},{4,60},{5,61},{6,62},{7,63},{8,0},{9,1... | collective-permute-start | bytes 393224 | tf_op jit(solution)/shard_map/ppermute | solution.py:323
  30.9 2.7 %collective-permute-start.9 = (bf16[2,32,1024]{2,1,0:T(8,128)(2,1)S(1)}, bf16[2,32,1024]{2,1,0:T(8,128)(2,1)S(1)}, u32[]{:S(2)}, u32[]{:S(2)}) collective-permute-start(bf16[2,32,1024]{2,1,0:T(8,128)(2,1)S(1)} %collective-permute-done.8), channel_id=1, source_target_pairs={{0,56},{1,57},{2,58},{3,59},{4,60},{5,61},{6,62},{7,63},{8,0},{9,1... | collective-permute-start | bytes 393224 | tf_op jit(solution)/shard_map/ppermute | solution.py:323
  35.9 3.0 %collective-permute-start.10 = (bf16[1,32,1024]{2,1,0:T(8,128)(2,1)S(1)}, bf16[1,32,1024]{2,1,0:T(8,128)(2,1)S(1)}, u32[]{:S(2)}, u32[]{:S(2)}) collective-permute-start(bf16[1,32,1024]{2,1,0:T(8,128)(2,1)S(1)} %slice.25), channel_id=1, source_target_pairs={{0,56},{1,57},{2,58},{3,59},{4,60},{5,61},{6,62},{7,63},{8,0},{9,1... | collective-permute-start | bytes 196616 | tf_op jit(solution)/shard_map/ppermute | solution.py:323
  43.0 2.0 %collective-permute-done.5 = bf16[1,32,1024]{2,1,0:T(8,128)(2,1)S(1)} collective-permute-done((bf16[1,32,1024]{2,1,0:T(8,128)(2,1)S(1)}, bf16[1,32,1024]{2,1,0:T(8,128)(2,1)S(1)}, u32[]{:S(2)}, u32[]{:S(2)}) %collective-permute-start.5) | collective-permute-done | bytes 65568 | tf_op jit(solution)/shard_map/ppermute | solution.py:323
  45.0 6.1 %all-to-all-start = ((bf16[64,4,16,128]{3,2,1,0:T(8,128)(2,1)}), bf16[64,4,16,128]{3,2,1,0:T(8,128)(2,1)S(1)}, u32[]{:S(2)}, u32[]{:S(2)}) async-start(bf16[64,4,16,128]{3,2,1,0:T(8,128)(2,1)} %bitcast.20), calls=%async_computation | async-start | bytes 2097152 | tf_op jit(solution)/shard_map/all_to_all | solution.py:364
  55.4 1.7 collective-permute-start.19
  57.2 2.7 %collective-permute-start.18 = (bf16[1,96,1024]{2,1,0:T(8,128)(2,1)S(1)}, bf16[1,96,1024]{2,1,0:T(8,128)(2,1)}, u32[]{:S(2)}, u32[]{:S(2)}) collective-permute-start(bf16[1,96,1024]{2,1,0:T(8,128)(2,1)S(1)} %slice.27), channel_id=1, source_target_pairs={{0,192},{1,193},{2,194},{3,195},{4,196},{5,197},{6,198},{7,199},{8... | collective-permute-start | bytes 589832 | tf_op jit(solution)/shard_map/ppermute | solution.py:323
  61.3 8.5 %collective-permute-start.13 = (bf16[5,32,128]{2,1,0:T(8,128)(2,1)}, bf16[5,32,128]{2,1,0:T(8,128)(2,1)S(1)}, u32[]{:S(2)}, u32[]{:S(2)}) collective-permute-start(bf16[5,32,128]{2,1,0:T(8,128)(2,1)} %pack.1.rest_0_), channel_id=1, source_target_pairs={{0,3},{1,2},{2,1},{3,0},{4,7},{5,6},{6,5},{7,4},{8,11},{9,10},{10,... | collective-permute-start | bytes 122888 | tf_op jit(solution)/shard_map/ppermute | solution.py:358
  69.8 3.0 %collective-permute-done.13.rest_3_ = bf16[5,32,128]{2,1,0:T(8,128)(2,1)S(1)} collective-permute-done((bf16[5,32,128]{2,1,0:T(8,128)(2,1)}, bf16[5,32,128]{2,1,0:T(8,128)(2,1)S(1)}, u32[]{:S(2)}, u32[]{:S(2)}) %collective-permute-start.13) | collective-permute-done | bytes 40992 | tf_op jit(solution)/shard_map/ppermute | solution.py:358
  75.3 2.3 %collective-permute-done.11.rest_1_ = bf16[5,32,128]{2,1,0:T(8,128)(2,1)S(1)} collective-permute-done((bf16[5,32,128]{2,1,0:T(8,128)(2,1)}, bf16[5,32,128]{2,1,0:T(8,128)(2,1)S(1)}, u32[]{:S(2)}, u32[]{:S(2)}) %collective-permute-start.11) | collective-permute-done | bytes 40992 | tf_op jit(solution)/shard_map/ppermute | solution.py:358
  79.1 5.4 %collective-permute-done.17.rest_6_ = bf16[1,96,1024]{2,1,0:T(8,128)(2,1)} collective-permute-done((bf16[1,96,1024]{2,1,0:T(8,128)(2,1)S(1)}, bf16[1,96,1024]{2,1,0:T(8,128)(2,1)}, u32[]{:S(2)}, u32[]{:S(2)}) %collective-permute-start.17) | collective-permute-done | bytes 196640 | tf_op jit(solution)/shard_map/ppermute | solution.py:323
  84.5 3.1 %collective-permute-start.27 = (bf16[2,96,1024]{2,1,0:T(8,128)(2,1)S(1)}, bf16[2,96,1024]{2,1,0:T(8,128)(2,1)S(1)}, u32[]{:S(2)}, u32[]{:S(2)}) collective-permute-start(bf16[2,96,1024]{2,1,0:T(8,128)(2,1)S(1)} %collective-permute-done.16.rest_8_), channel_id=1, source_target_pairs={{0,1},{1,0},{2,3},{3,2},{4,5},{5,4},{6,7},{7,6},{8,9},{9,8},{10,11... | collective-permute-start | bytes 1179656 | tf_op jit(solution)/shard_map/ppermute | solution.py:344
  89.9 11.6 %collective-permute-start.21 = (bf16[1,160,1024]{2,1,0:T(8,128)(2,1)S(1)}, bf16[1,160,1024]{2,1,0:T(8,128)(2,1)}, u32[]{:S(2)}, u32[]{:S(2)}) collective-permute-start(bf16[1,160,1024]{2,1,0:T(8,128)(2,1)S(1)} %slice.28), channel_id=1, source_target_pairs={{0,64},{1,65},{2,66},{3,67},{4,68},{5,69},{6,70},{7,71},{8,72},{9,... | collective-permute-start | bytes 983048 | tf_op jit(solution)/shard_map/ppermute | solution.py:323
  101.6 2.6 %collective-permute-start.22 = (bf16[1,160,1024]{2,1,0:T(8,128)(2,1)S(1)}, bf16[1,160,1024]{2,1,0:T(8,128)(2,1)}, u32[]{:S(2)}, u32[]{:S(2)}) collective-permute-start(bf16[1,160,1024]{2,1,0:T(8,128)(2,1)S(1)} %slice.29), channel_id=1, source_target_pairs={{0,192},{1,193},{2,194},{3,195},{4,196},{5,197},{6,198},{7,199},{8... | collective-permute-start | bytes 983048 | tf_op jit(solution)/shard_map/ppermute | solution.py:323
  105.1 6.8 %collective-permute-done.21.rest_11_ = bf16[1,160,1024]{2,1,0:T(8,128)(2,1)} collective-permute-done((bf16[1,160,1024]{2,1,0:T(8,128)(2,1)S(1)}, bf16[1,160,1024]{2,1,0:T(8,128)(2,1)}, u32[]{:S(2)}, u32[]{:S(2)}) %collective-permute-start.21) | collective-permute-done | bytes 327712 | tf_op jit(solution)/shard_map/ppermute | solution.py:323
  116.0 30.0 %attend.1 = bf16[4,1024,128]{2,1,0:T(8,128)(2,1)} custom-call(s32[3]{0:T(128)} %copy-done, s32[1]{0:T(128)} %bitcast.3.upper_ref, bf16[64,4,16,128]{3,2,1,0:T(8,128)(2,1)} %copy-done.4, bf16[4,256,128]{2,1,0:T(8,128)(2,1)} %copy-done.3, bf16[4,256,1024]{2,1,0:T(8,128)(2,1)} %copy-done.2, bf16[5,32,128]{2,1,0:T(8,128)(2,1)} %pack.1.rest_0_, ...), custom_call_target="tpu_custom_call" | custom-call | flops 44000002048 | tf_op jit(solution)/shard_map/attend/pallas_call | solution.py:283
  146.0 41.9 %all_to_all.10 = bf16[256,16,128]{2,1,0:T(8,128)(2,1)S(1)} all-to-all(bf16[256,16,128]{2,1,0:T(8,128)(2,1)} %bitcast.22), channel_id=1, replica_groups=mesh['dap'=64,'head'=4] {'head','dap'}, dimensions={0} | all-to-all | bytes 2097152 | tf_op jit(solution)/shard_map/all_to_all | solution.py:367
  (115 shorter events, 32.0 us)
Async XLA Ops:
  0.0 12.8 %collective-permute-start = (bf16[1,128]{1,0:T(2,128)(2,1)}, bf16[1,128]{1,0:T(2,128)(2,1)S(1)}, u32[]{:S(2)}, u32[]{:S(2)}) collective-permute-start(bf16[1,128]{1,0:T(2,128)(2,1)} %bitcast.23), channel_id=1, source_target_pairs={{0,2},{1,3},{2,0},{3,1},{4,6},{5,7},{6,4},{7,5},{8,10},{9,11},{10,... | collective-permute-start | bytes 776 | tf_op jit(solution)/shard_map/ppermute | solution.py:352
  14.0 15.6 %collective-permute-start.14 = (bf16[2,16,1024]{2,1,0:T(8,128)(2,1)S(1)}, bf16[2,16,1024]{2,1,0:T(8,128)(2,1)S(1)}, u32[]{:S(2)}, u32[]{:S(2)}) collective-permute-start(bf16[2,16,1024]{2,1,0:T(8,128)(2,1)S(1)} %bias.1), channel_id=1, source_target_pairs={{0,6},{1,7},{2,4},{3,5},{4,2},{5,3},{6,0},{7,1},{8,14},{9,15},{10,... | collective-permute-start | bytes 196616 | tf_op jit(solution)/shard_map/ppermute | solution.py:323
  16.0 9.8 %collective-permute-start.7 = (bf16[2,16,1024]{2,1,0:T(8,128)(2,1)S(1)}, bf16[2,16,1024]{2,1,0:T(8,128)(2,1)S(1)}, u32[]{:S(2)}, u32[]{:S(2)}) collective-permute-start(bf16[2,16,1024]{2,1,0:T(8,128)(2,1)S(1)} %bias.1), channel_id=1, source_target_pairs={{0,62},{1,63},{2,60},{3,61},{4,58},{5,59},{6,56},{7,57},{8,6},{9,7... | collective-permute-start | bytes 196616 | tf_op jit(solution)/shard_map/ppermute | solution.py:323
  22.8 6.4 %collective-permute-start.2 = (bf16[2,16,1024]{2,1,0:T(8,128)(2,1)S(1)}, bf16[2,16,1024]{2,1,0:T(8,128)(2,1)S(1)}, u32[]{:S(2)}, u32[]{:S(2)}) collective-permute-start(bf16[2,16,1024]{2,1,0:T(8,128)(2,1)S(1)} %bias.1), channel_id=1, source_target_pairs={{0,14},{1,15},{2,12},{3,13},{4,10},{5,11},{6,8},{7,9},{8,22},{9,23... | collective-permute-start | bytes 196616 | tf_op jit(solution)/shard_map/ppermute | solution.py:323
  29.5 5.1 %collective-permute-start.3 = (bf16[2,32,1024]{2,1,0:T(8,128)(2,1)S(1)}, bf16[2,32,1024]{2,1,0:T(8,128)(2,1)S(1)}, u32[]{:S(2)}, u32[]{:S(2)}) collective-permute-start(bf16[2,32,1024]{2,1,0:T(8,128)(2,1)S(1)} %pad_maximum_fusion), channel_id=1, source_target_pairs={{0,8},{1,9},{2,10},{3,11},{4,12},{5,13},{6,14},{7,15},{8,16},{9,17... | collective-permute-start | bytes 393224 | tf_op jit(solution)/shard_map/ppermute | solution.py:323
  35.9 7.2 %collective-permute-start.10 = (bf16[1,32,1024]{2,1,0:T(8,128)(2,1)S(1)}, bf16[1,32,1024]{2,1,0:T(8,128)(2,1)S(1)}, u32[]{:S(2)}, u32[]{:S(2)}) collective-permute-start(bf16[1,32,1024]{2,1,0:T(8,128)(2,1)S(1)} %slice.25), channel_id=1, source_target_pairs={{0,56},{1,57},{2,58},{3,59},{4,60},{5,61},{6,62},{7,63},{8,0},{9,1... | collective-permute-start | bytes 196616 | tf_op jit(solution)/shard_map/ppermute | solution.py:323
  39.7 5.3 %collective-permute-start.5 = (bf16[1,32,1024]{2,1,0:T(8,128)(2,1)S(1)}, bf16[1,32,1024]{2,1,0:T(8,128)(2,1)S(1)}, u32[]{:S(2)}, u32[]{:S(2)}) collective-permute-start(bf16[1,32,1024]{2,1,0:T(8,128)(2,1)S(1)} %slice.24), channel_id=1, source_target_pairs={{0,8},{1,9},{2,10},{3,11},{4,12},{5,13},{6,14},{7,15},{8,16},{9,17... | collective-permute-start | bytes 196616 | tf_op jit(solution)/shard_map/ppermute | solution.py:323
  40.4 16.7 %collective-permute-start.16 = (bf16[2,96,1024]{2,1,0:T(8,128)(2,1)}, bf16[2,96,1024]{2,1,0:T(8,128)(2,1)S(1)}, u32[]{:S(2)}, u32[]{:S(2)}) collective-permute-start(bf16[2,96,1024]{2,1,0:T(8,128)(2,1)} %constant_dynamic-update-slice_fusion.rest_4_), channel_id=1, source_target_pairs={{0,64},{1,65},{2,66},{3,67},{4,68},{5,69},{6,70},{7,71},{8,72},{9,... | collective-permute-start | bytes 1179656 | tf_op jit(solution)/shard_map/ppermute | solution.py:323
  41.6 15.6 %collective-permute-start.15 = (bf16[2,96,1024]{2,1,0:T(8,128)(2,1)}, bf16[2,96,1024]{2,1,0:T(8,128)(2,1)S(1)}, u32[]{:S(2)}, u32[]{:S(2)}) collective-permute-start(bf16[2,96,1024]{2,1,0:T(8,128)(2,1)} %constant_dynamic-update-slice_fusion.rest_4_), channel_id=1, source_target_pairs={{0,192},{1,193},{2,194},{3,195},{4,196},{5,197},{6,198},{7,199},{8... | collective-permute-start | bytes 1179656 | tf_op jit(solution)/shard_map/ppermute | solution.py:323
  45.0 70.0 %all-to-all-start = ((bf16[64,4,16,128]{3,2,1,0:T(8,128)(2,1)}), bf16[64,4,16,128]{3,2,1,0:T(8,128)(2,1)S(1)}, u32[]{:S(2)}, u32[]{:S(2)}) async-start(bf16[64,4,16,128]{3,2,1,0:T(8,128)(2,1)} %bitcast.20), calls=%async_computation | async-start | bytes 2097152 | tf_op jit(solution)/shard_map/all_to_all | solution.py:364
  54.4 33.3 %collective-permute-start.20 = (bf16[2,160,1024]{2,1,0:T(8,128)(2,1)}, bf16[2,160,1024]{2,1,0:T(8,128)(2,1)S(1)}, u32[]{:S(2)}, u32[]{:S(2)}) collective-permute-start(bf16[2,160,1024]{2,1,0:T(8,128)(2,1)} %maximum_dynamic-update-slice_fusion.rest_9_), channel_id=1, source_target_pairs={{0,64},{1,65},{2,66},{3,67},{4,68},{5,69},{6,70},{7,71},{8,72},{9,... | collective-permute-start | bytes 1966088 | tf_op jit(solution)/shard_map/ppermute | solution.py:323
  55.4 32.8 %collective-permute-start.19 = (bf16[2,160,1024]{2,1,0:T(8,128)(2,1)}, bf16[2,160,1024]{2,1,0:T(8,128)(2,1)S(1)}, u32[]{:S(2)}, u32[]{:S(2)}) collective-permute-start(bf16[2,160,1024]{2,1,0:T(8,128)(2,1)} %maximum_dynamic-update-slice_fusion.rest_9_), channel_id=1, source_target_pairs={{0,192},{1,193},{2,194},{3,195},{4,196},{5,197},{6,198},{7,199},{8... | collective-permute-start | bytes 1966088 | tf_op jit(solution)/shard_map/ppermute | solution.py:323
  57.1 27.4 %collective-permute-start.17 = (bf16[1,96,1024]{2,1,0:T(8,128)(2,1)S(1)}, bf16[1,96,1024]{2,1,0:T(8,128)(2,1)}, u32[]{:S(2)}, u32[]{:S(2)}) collective-permute-start(bf16[1,96,1024]{2,1,0:T(8,128)(2,1)S(1)} %slice.26), channel_id=1, source_target_pairs={{0,64},{1,65},{2,66},{3,67},{4,68},{5,69},{6,70},{7,71},{8,72},{9,... | collective-permute-start | bytes 589832 | tf_op jit(solution)/shard_map/ppermute | solution.py:323
  57.2 30.4 %collective-permute-start.18 = (bf16[1,96,1024]{2,1,0:T(8,128)(2,1)S(1)}, bf16[1,96,1024]{2,1,0:T(8,128)(2,1)}, u32[]{:S(2)}, u32[]{:S(2)}) collective-permute-start(bf16[1,96,1024]{2,1,0:T(8,128)(2,1)S(1)} %slice.27), channel_id=1, source_target_pairs={{0,192},{1,193},{2,194},{3,195},{4,196},{5,197},{6,198},{7,199},{8... | collective-permute-start | bytes 589832 | tf_op jit(solution)/shard_map/ppermute | solution.py:323
  61.3 11.5 %collective-permute-start.13 = (bf16[5,32,128]{2,1,0:T(8,128)(2,1)}, bf16[5,32,128]{2,1,0:T(8,128)(2,1)S(1)}, u32[]{:S(2)}, u32[]{:S(2)}) collective-permute-start(bf16[5,32,128]{2,1,0:T(8,128)(2,1)} %pack.1.rest_0_), channel_id=1, source_target_pairs={{0,3},{1,2},{2,1},{3,0},{4,7},{5,6},{6,5},{7,4},{8,11},{9,10},{10,... | collective-permute-start | bytes 122888 | tf_op jit(solution)/shard_map/ppermute | solution.py:358
  77.6 10.8 %collective-permute-start.23 = (bf16[2,96,1024]{2,1,0:T(8,128)(2,1)}, bf16[2,96,1024]{2,1,0:T(8,128)(2,1)S(1)}, u32[]{:S(2)}, u32[]{:S(2)}) collective-permute-start(bf16[2,96,1024]{2,1,0:T(8,128)(2,1)} %constant_dynamic-update-slice_fusion.rest_4_), channel_id=1, source_target_pairs={{0,1},{1,0},{2,3},{3,2},{4,5},{5,4},{6,7},{7,6},{8,9},{9,8},{10,11... | collective-permute-start | bytes 1179656 | tf_op jit(solution)/shard_map/ppermute | solution.py:344
  84.5 17.1 %collective-permute-start.27 = (bf16[2,96,1024]{2,1,0:T(8,128)(2,1)S(1)}, bf16[2,96,1024]{2,1,0:T(8,128)(2,1)S(1)}, u32[]{:S(2)}, u32[]{:S(2)}) collective-permute-start(bf16[2,96,1024]{2,1,0:T(8,128)(2,1)S(1)} %collective-permute-done.16.rest_8_), channel_id=1, source_target_pairs={{0,1},{1,0},{2,3},{3,2},{4,5},{5,4},{6,7},{7,6},{8,9},{9,8},{10,11... | collective-permute-start | bytes 1179656 | tf_op jit(solution)/shard_map/ppermute | solution.py:344
  87.6 17.4 %collective-permute-start.24 = (bf16[2,96,1024]{2,1,0:T(8,128)(2,1)S(1)}, bf16[2,96,1024]{2,1,0:T(8,128)(2,1)S(1)}, u32[]{:S(2)}, u32[]{:S(2)}) collective-permute-start(bf16[2,96,1024]{2,1,0:T(8,128)(2,1)S(1)} %collective-permute-done.15.rest_5_), channel_id=1, source_target_pairs={{0,1},{1,0},{2,3},{3,2},{4,5},{5,4},{6,7},{7,6},{8,9},{9,8},{10,11... | collective-permute-start | bytes 1179656 | tf_op jit(solution)/shard_map/ppermute | solution.py:344
  88.2 16.0 %collective-permute-start.26 = (bf16[1,96,1024]{2,1,0:T(8,128)(2,1)}, bf16[1,96,1024]{2,1,0:T(8,128)(2,1)S(1)}, u32[]{:S(2)}, u32[]{:S(2)}) collective-permute-start(bf16[1,96,1024]{2,1,0:T(8,128)(2,1)} %collective-permute-done.18.rest_7_), channel_id=1, source_target_pairs={{0,1},{1,0},{2,3},{3,2},{4,5},{5,4},{6,7},{7,6},{8,9},{9,8},{10,11... | collective-permute-start | bytes 589832 | tf_op jit(solution)/shard_map/ppermute | solution.py:344
  88.4 24.7 %collective-permute-start.28 = (bf16[2,160,1024]{2,1,0:T(8,128)(2,1)}, bf16[2,160,1024]{2,1,0:T(8,128)(2,1)}, u32[]{:S(2)}, u32[]{:S(2)}) collective-permute-start(bf16[2,160,1024]{2,1,0:T(8,128)(2,1)} %maximum_dynamic-update-slice_fusion.rest_9_), channel_id=1, source_target_pairs={{0,1},{1,0},{2,3},{3,2},{4,5},{5,4},{6,7},{7,6},{8,9},{9,8},{10,11... | collective-permute-start | bytes 1966088 | tf_op jit(solution)/shard_map/ppermute | solution.py:344
  89.9 22.0 %collective-permute-start.21 = (bf16[1,160,1024]{2,1,0:T(8,128)(2,1)S(1)}, bf16[1,160,1024]{2,1,0:T(8,128)(2,1)}, u32[]{:S(2)}, u32[]{:S(2)}) collective-permute-start(bf16[1,160,1024]{2,1,0:T(8,128)(2,1)S(1)} %slice.28), channel_id=1, source_target_pairs={{0,64},{1,65},{2,66},{3,67},{4,68},{5,69},{6,70},{7,71},{8,72},{9,... | collective-permute-start | bytes 983048 | tf_op jit(solution)/shard_map/ppermute | solution.py:323
  101.6 11.4 %collective-permute-start.22 = (bf16[1,160,1024]{2,1,0:T(8,128)(2,1)S(1)}, bf16[1,160,1024]{2,1,0:T(8,128)(2,1)}, u32[]{:S(2)}, u32[]{:S(2)}) collective-permute-start(bf16[1,160,1024]{2,1,0:T(8,128)(2,1)S(1)} %slice.29), channel_id=1, source_target_pairs={{0,192},{1,193},{2,194},{3,195},{4,196},{5,197},{6,198},{7,199},{8... | collective-permute-start | bytes 983048 | tf_op jit(solution)/shard_map/ppermute | solution.py:323
  104.2 10.4 %collective-permute-start.32 = (bf16[2,160,1024]{2,1,0:T(8,128)(2,1)S(1)}, bf16[2,160,1024]{2,1,0:T(8,128)(2,1)}, u32[]{:S(2)}, u32[]{:S(2)}) collective-permute-start(bf16[2,160,1024]{2,1,0:T(8,128)(2,1)S(1)} %collective-permute-done.20.rest_13_), channel_id=1, source_target_pairs={{0,1},{1,0},{2,3},{3,2},{4,5},{5,4},{6,7},{7,6},{8,9},{9,8},{10,11... | collective-permute-start | bytes 1966088 | tf_op jit(solution)/shard_map/ppermute | solution.py:344
  105.0 10.1 %collective-permute-start.29 = (bf16[2,160,1024]{2,1,0:T(8,128)(2,1)S(1)}, bf16[2,160,1024]{2,1,0:T(8,128)(2,1)}, u32[]{:S(2)}, u32[]{:S(2)}) collective-permute-start(bf16[2,160,1024]{2,1,0:T(8,128)(2,1)S(1)} %collective-permute-done.19.rest_10_), channel_id=1, source_target_pairs={{0,1},{1,0},{2,3},{3,2},{4,5},{5,4},{6,7},{7,6},{8,9},{9,8},{10,11... | collective-permute-start | bytes 1966088 | tf_op jit(solution)/shard_map/ppermute | solution.py:344
  (28 other events, 352.7 us)
where the time goes:
time: 193 us; the launch traced here: 190 us
  starting transfers between devices  68.1 us (35%)
  blocking collectives  41.9 us (22%)
  Pallas kernels  39.5 us (20%)
  waiting for transfers between devices  26.3 us (14%)
  local copies, waits for them, and re-layouts  12.8 us (7%)
    ppermute x19, starting transfers between devices, send(): return lax.ppermute(value, ('dap', 'head'), pairs)  42.2 us
    all_to_all x1, blocking collectives, body(): update = lax.all_to_all(update, ('head', 'dap'), 0, 0, tiled=True)  41.9 us
    pallas_call x1, Pallas kernels, attend_call(): pl.pallas_call(attend_kernel, grid=(N // TILE,), in_specs=[pl.BlockSpec(m...  30 us
    ppermute x19, waiting for transfers between devices, send(): return lax.ppermute(value, ('dap', 'head'), pairs)  17 us
    ppermute x3, starting transfers between devices, body(): lax.ppermute(mine, 'head', [(h, h ^ n) for h in range(HEADS)])  9.92 us
    ppermute x10, starting transfers between devices, gather_bias(): return (own + [lax.ppermute(piece, 'head', swap) for piece in own], out)  7.82 us
    unnamed x45, local copies, waits for them, and re-layouts  6.73 us
    ppermute x3, waiting for transfers between devices, body(): lax.ppermute(mine, 'head', [(h, h ^ n) for h in range(HEADS)])  6.35 us
  transfers between devices with their start and end apart: 34, of which 13 were waited for; matrix products, arithmetic and copies ran while one was open for 6% of the time, Pallas kernels for 4%

commit v1 on v0

--- a/solution.py
+++ b/solution.py
@@ -207,8 +207,8 @@
 def attend_kernel(
     place_ref, upper_ref, recv_ref, keep_ref, extra_ref, *rest
 ):
-    parts, bias_refs = rest[:4], rest[4:24]
-    out_ref, w_ref, wout_ref, k_ref, q_ref, v_ref, g_ref, comb, s_scr, gated = rest[24:]
+    parts, bias_refs = rest[:4], rest[4:14]
+    out_ref, w_ref, wout_ref, k_ref, q_ref, v_ref, g_ref, comb, s_scr, gated = rest[14:]
     lanes = pl.ds(pl.multiple_of(pl.program_id(0) * TILE, TILE), TILE)
 
     @pl.when(pl.program_id(0) == 0)
@@ -225,10 +225,8 @@
     zeros = jnp.zeros((2 * WIDTH, TILE), bf16)
 
     def bias(h, s):
-        parts = bias_refs[10 * (h // 2) : 10 * (h // 2) + 10]
-        if s == 2:
-            return [parts[2 + 5 * group + h % 2][0] for group in range(2)]
-        return [parts[(0, 1, None, 4)[s] + 5 * group][h % 2] for group in range(2)]
+        parts = bias_refs[5 * (h // 2) : 5 * (h // 2) + 5]
+        return [parts[2 + h % 2][0] if s == 2 else parts[s if s < 2 else 4][h % 2]]
 
     def score(h, c, s, q, top):
         k = k_ref[c, h // 2, s * chunk : (s + 1) * chunk]
@@ -335,11 +333,9 @@
     last = [send(up[:1], 0, 1), send(down[1:], 0, -1)]
     out, *last = lax.optimization_barrier((out, *last))
     last = jnp.concatenate(last, 0)
-    far = jnp.concatenate(got + [last], 1)
-    own = []
-    for group in (near, far):
-        left, right = send(group, 1, 0), send(group, -1, 0)
-        own += [group, right, send(left[:1], 1, 0), send(right[1:], -1, 0), left]
+    plane = jnp.concatenate([near] + got + [last], 1)
+    left, right = send(plane, 1, 0), send(plane, -1, 0)
+    own = [plane, right, send(left[:1], 1, 0), send(right[1:], -1, 0), left]
     swap = [(h, h ^ 1) for h in range(HEADS)]
     return own + [lax.ppermute(piece, "head", swap) for piece in own], out
 
@@ -356,7 +352,7 @@
     )
     mine = pack_call(w_query.T, w_key.T, w_value.T, w_gate.T, w_out)
     parts = [mine] + [lax.ppermute(mine, "head", [(h, h ^ n) for h in range(HEADS)]) for n in (2, 1, 3)]
-    wide = lambda v: jnp.broadcast_to(v[None], (8, N))
+    wide = lambda v: v.reshape(1, N)
     extra, keep = mask_call(place, wide(residue_mask), wide(chain_breaks))
     which, extra, keep = lax.optimization_barrier((head[None], extra, keep))
     normed, out = norm_call(pair, which)

time: 193 us -> 172 us (0.89); the launches traced: 190 us -> 172 us
  starting transfers between devices: 68.1 us -> 53.6 us
  blocking collectives: 41.9 us -> 36.8 us
    ppermute x19 -> x15, starting transfers between devices: 42.2 us -> 25.3 us  [send(): return lax.ppermute(value, ('dap', 'head'), pairs)]
    ppermute x19 -> x15, waiting for transfers between devices: 17 us -> 25.3 us  [send(): return lax.ppermute(value, ('dap', 'head'), pairs)]
    ppermute x3, waiting for transfers between devices: 6.35 us -> 0.01 us  [body(): lax.ppermute(mine, 'head', [(h, h ^ n) for h in range(HEADS)])]
    ppermute x10 -> x5, starting transfers between devices: 7.82 us -> 13.8 us  [gather_bias(): return (own + [lax.ppermute(piece, 'head', swap) for piece in own], out)]
    all_to_all x1, blocking collectives: 41.9 us -> 36.8 us  [body(): update = lax.all_to_all(update, ('head', 'dap'), 0, 0, tiled=True)]
    ppermute x3, starting transfers between devices: 9.92 us -> 7.6 us  [body(): lax.ppermute(mine, 'head', [(h, h ^ n) for h in range(HEADS)])]
    unnamed x45 -> x36, local copies, waits for them, and re-layouts: 6.73 us -> 8.18 us
  transfers between devices with their start and end apart: 34 -> 25, of which waited for: 13 -> 9; matrix products, arithmetic and copies ran while one was open for 6% -> 5% of each run, Pallas kernels for 4% -> 5%
where the time goes in v1:
time: 172 us
  starting transfers between devices  53.6 us (31%)
  Pallas kernels  40.1 us (23%)
  blocking collectives  36.8 us (21%)
  waiting for transfers between devices  27.9 us (16%)
  local copies, waits for them, and re-layouts  11.9 us (7%)
    all_to_all x1, blocking collectives, body(): update = lax.all_to_all(update, ('head', 'dap'), 0, 0, tiled=True)  36.8 us
    pallas_call x1, Pallas kernels, attend_call(): pl.pallas_call(attend_kernel, grid=(N // TILE,), in_specs=[pl.BlockSpec(m...  30.6 us
    ppermute x15, waiting for transfers between devices, send(): return lax.ppermute(value, ('dap', 'head'), pairs)  25.3 us
    ppermute x15, starting transfers between devices, send(): return lax.ppermute(value, ('dap', 'head'), pairs)  25.3 us
    ppermute x5, starting transfers between devices, gather_bias(): return (own + [lax.ppermute(piece, 'head', swap) for piece in own], out)  13.8 us
    unnamed x36, local copies, waits for them, and re-layouts  8.18 us
    ppermute x3, starting transfers between devices, body(): lax.ppermute(mine, 'head', [(h, h ^ n) for h in range(HEADS)])  7.6 us
    all_to_all x1, starting transfers between devices, body(): recv = lax.all_to_all(out, 'dap', 0, 0, tiled=True)  4.84 us
  transfers between devices with their start and end apart: 25, of which 9 were waited for; matrix products, arithmetic and copies ran while one was open for 5% of the time, Pallas kernels for 5%

profile of v1, /device:TPU:1, one launch (start us, length us, event | category | flops | bytes accessed | tf_op | source)
XLA Modules:
  0.0 171.5 jit_solution(8546740730184362984)
XLA Ops:
  0.0 2.1 %collective-permute-start = (bf16[1,128]{1,0:T(2,128)(2,1)}, bf16[1,128]{1,0:T(2,128)(2,1)S(1)}, u32[]{:S(2)}, u32[]{:S(2)}) collective-permute-start(bf16[1,128]{1,0:T(2,128)(2,1)} %bitcast.27), channel_id=1, source_target_pairs={{0,2},{1,3},{2,0},{3,1},{4,6},{5,7},{6,4},{7,5},{8,10},{9,11},{10,... | collective-permute-start | bytes 776 | tf_op jit(solution)/shard_map/ppermute | solution.py:348
  4.0 2.4 %mask.1 = (bf16[4,256,1024]{2,1,0:T(8,128)(2,1)S(1)}, bf16[4,256,128]{2,1,0:T(8,128)(2,1)S(1)}) custom-call(s32[3]{0:T(128)S(1)} %pad_add_fusion.place_ref, s32[1,1024]{1,0:T(1,128)S(1)} %bitcast.23, s32[1,1024]{1,0:T(1,128)S(1)} %bitcast.24), custom_call_target="tpu_custom_call" | custom-call | flops 2200000000 | tf_op jit(solution)/shard_map/mask/pallas_call | solution.py:142
  6.4 4.6 %norm.1 = (bf16[16,1024,128]{2,1,0:T(8,128)(2,1)S(1)}, bf16[4,16,64,128]{3,2,1,0:T(8,128)(2,1)S(1)}) custom-call(s32[1]{0:T(128)} %bitcast.4.head_ref, bf16[16,1024,128]{2,1,0:T(8,128)(2,1)S(1)} %copy-done.1), custom_call_target="tpu_custom_call" | custom-call | flops 6600000000 | bytes 9437184 | tf_op jit(solution)/shard_map/norm/pallas_call | solution.py:52
  11.0 1.6 copy.22
  12.8 1.2 bias.1
  14.0 2.0 %collective-permute-start.14 = (bf16[2,16,1024]{2,1,0:T(8,128)(2,1)S(1)}, bf16[2,16,1024]{2,1,0:T(8,128)(2,1)S(1)}, u32[]{:S(2)}, u32[]{:S(2)}) collective-permute-start(bf16[2,16,1024]{2,1,0:T(8,128)(2,1)S(1)} %bias.1), channel_id=1, source_target_pairs={{0,6},{1,7},{2,4},{3,5},{4,2},{5,3},{6,0},{7,1},{8,14},{9,15},{10,... | collective-permute-start | bytes 196616 | tf_op jit(solution)/shard_map/ppermute | solution.py:321
  16.0 6.1 %collective-permute-start.7 = (bf16[2,16,1024]{2,1,0:T(8,128)(2,1)S(1)}, bf16[2,16,1024]{2,1,0:T(8,128)(2,1)S(1)}, u32[]{:S(2)}, u32[]{:S(2)}) collective-permute-start(bf16[2,16,1024]{2,1,0:T(8,128)(2,1)S(1)} %bias.1), channel_id=1, source_target_pairs={{0,62},{1,63},{2,60},{3,61},{4,58},{5,59},{6,56},{7,57},{8,6},{9,7... | collective-permute-start | bytes 196616 | tf_op jit(solution)/shard_map/ppermute | solution.py:321
  22.8 2.4 %collective-permute-start.2 = (bf16[2,16,1024]{2,1,0:T(8,128)(2,1)S(1)}, bf16[2,16,1024]{2,1,0:T(8,128)(2,1)S(1)}, u32[]{:S(2)}, u32[]{:S(2)}) collective-permute-start(bf16[2,16,1024]{2,1,0:T(8,128)(2,1)S(1)} %bias.1), channel_id=1, source_target_pairs={{0,14},{1,15},{2,12},{3,13},{4,10},{5,11},{6,8},{7,9},{8,22},{9,23... | collective-permute-start | bytes 196616 | tf_op jit(solution)/shard_map/ppermute | solution.py:321
  25.8 2.7 %collective-permute-start.8 = (bf16[2,32,1024]{2,1,0:T(8,128)(2,1)S(1)}, bf16[2,32,1024]{2,1,0:T(8,128)(2,1)S(1)}, u32[]{:S(2)}, u32[]{:S(2)}) collective-permute-start(bf16[2,32,1024]{2,1,0:T(8,128)(2,1)S(1)} %pad_maximum_fusion.1), channel_id=1, source_target_pairs={{0,56},{1,57},{2,58},{3,59},{4,60},{5,61},{6,62},{7,63},{8,0},{9,1... | collective-permute-start | bytes 393224 | tf_op jit(solution)/shard_map/ppermute | solution.py:321
  32.7 2.7 %collective-permute-start.9 = (bf16[2,32,1024]{2,1,0:T(8,128)(2,1)S(1)}, bf16[2,32,1024]{2,1,0:T(8,128)(2,1)S(1)}, u32[]{:S(2)}, u32[]{:S(2)}) collective-permute-start(bf16[2,32,1024]{2,1,0:T(8,128)(2,1)S(1)} %collective-permute-done.8), channel_id=1, source_target_pairs={{0,56},{1,57},{2,58},{3,59},{4,60},{5,61},{6,62},{7,63},{8,0},{9,1... | collective-permute-start | bytes 393224 | tf_op jit(solution)/shard_map/ppermute | solution.py:321
  37.4 3.1 %collective-permute-start.10 = (bf16[1,32,1024]{2,1,0:T(8,128)(2,1)S(1)}, bf16[1,32,1024]{2,1,0:T(8,128)(2,1)S(1)}, u32[]{:S(2)}, u32[]{:S(2)}) collective-permute-start(bf16[1,32,1024]{2,1,0:T(8,128)(2,1)S(1)} %slice.17), channel_id=1, source_target_pairs={{0,56},{1,57},{2,58},{3,59},{4,60},{5,61},{6,62},{7,63},{8,0},{9,1... | collective-permute-start | bytes 196616 | tf_op jit(solution)/shard_map/ppermute | solution.py:321
  42.0 3.5 %collective-permute-done.5 = bf16[1,32,1024]{2,1,0:T(8,128)(2,1)S(1)} collective-permute-done((bf16[1,32,1024]{2,1,0:T(8,128)(2,1)S(1)}, bf16[1,32,1024]{2,1,0:T(8,128)(2,1)S(1)}, u32[]{:S(2)}, u32[]{:S(2)}) %collective-permute-start.5) | collective-permute-done | bytes 65568 | tf_op jit(solution)/shard_map/ppermute | solution.py:321
  46.2 1.2 collective-permute-start.16
  47.4 1.5 collective-permute-start.15
  48.9 4.8 %all-to-all-start = ((bf16[64,4,16,128]{3,2,1,0:T(8,128)(2,1)}), bf16[64,4,16,128]{3,2,1,0:T(8,128)(2,1)S(1)}, u32[]{:S(2)}, u32[]{:S(2)}) async-start(bf16[64,4,16,128]{3,2,1,0:T(8,128)(2,1)} %bitcast.22), calls=%async_computation | async-start | bytes 2097152 | tf_op jit(solution)/shard_map/all_to_all | solution.py:360
  53.7 1.4 pack.1.rest_0_
  55.1 7.1 %collective-permute-start.13 = (bf16[5,32,128]{2,1,0:T(8,128)(2,1)}, bf16[5,32,128]{2,1,0:T(8,128)(2,1)S(1)}, u32[]{:S(2)}, u32[]{:S(2)}) collective-permute-start(bf16[5,32,128]{2,1,0:T(8,128)(2,1)} %pack.1.rest_0_), channel_id=1, source_target_pairs={{0,3},{1,2},{2,1},{3,0},{4,7},{5,6},{6,5},{7,4},{8,11},{9,10},{10,... | collective-permute-start | bytes 122888 | tf_op jit(solution)/shard_map/ppermute | solution.py:354
  62.7 8.7 %collective-permute-done.16.rest_8_ = bf16[2,256,1024]{2,1,0:T(8,128)(2,1)S(1)} collective-permute-done((bf16[2,256,1024]{2,1,0:T(8,128)(2,1)}, bf16[2,256,1024]{2,1,0:T(8,128)(2,1)S(1)}, u32[]{:S(2)}, u32[]{:S(2)}) %collective-permute-start.16) | collective-permute-done | bytes 1048608 | tf_op jit(solution)/shard_map/ppermute | solution.py:321
  71.4 12.3 %collective-permute-start.19 = (bf16[2,256,1024]{2,1,0:T(8,128)(2,1)}, bf16[2,256,1024]{2,1,0:T(8,128)(2,1)}, u32[]{:S(2)}, u32[]{:S(2)}) collective-permute-start(bf16[2,256,1024]{2,1,0:T(8,128)(2,1)} %maximum_dynamic-update-slice_fusion.rest_4_), channel_id=1, source_target_pairs={{0,1},{1,0},{2,3},{3,2},{4,5},{5,4},{6,7},{7,6},{8,9},{9,8},{10,11... | collective-permute-start | bytes 3145736 | tf_op jit(solution)/shard_map/ppermute | solution.py:340
  83.9 2.7 %collective-permute-start.18 = (bf16[1,256,1024]{2,1,0:T(8,128)(2,1)S(1)}, bf16[1,256,1024]{2,1,0:T(8,128)(2,1)}, u32[]{:S(2)}, u32[]{:S(2)}) collective-permute-start(bf16[1,256,1024]{2,1,0:T(8,128)(2,1)S(1)} %slice.19), channel_id=1, source_target_pairs={{0,192},{1,193},{2,194},{3,195},{4,196},{5,197},{6,198},{7,199},{8... | collective-permute-start | bytes 1572872 | tf_op jit(solution)/shard_map/ppermute | solution.py:321
  87.3 11.4 %collective-permute-done.17.rest_6_ = bf16[1,256,1024]{2,1,0:T(8,128)(2,1)} collective-permute-done((bf16[1,256,1024]{2,1,0:T(8,128)(2,1)S(1)}, bf16[1,256,1024]{2,1,0:T(8,128)(2,1)}, u32[]{:S(2)}, u32[]{:S(2)}) %collective-permute-start.17) | collective-permute-done | bytes 524320 | tf_op jit(solution)/shard_map/ppermute | solution.py:321
  99.5 1.8 %collective-permute-done.21.rest_11_ = bf16[1,256,1024]{2,1,0:T(8,128)(2,1)} collective-permute-done((bf16[1,256,1024]{2,1,0:T(8,128)(2,1)}, bf16[1,256,1024]{2,1,0:T(8,128)(2,1)}, u32[]{:S(2)}, u32[]{:S(2)}) %collective-permute-start.21) | collective-permute-done | bytes 524320 | tf_op jit(solution)/shard_map/ppermute | solution.py:340
  102.2 30.6 %attend.1 = bf16[4,1024,128]{2,1,0:T(8,128)(2,1)} custom-call(s32[3]{0:T(128)} %copy-done, s32[1]{0:T(128)} %bitcast.3.upper_ref, bf16[64,4,16,128]{3,2,1,0:T(8,128)(2,1)} %copy-done.6, bf16[4,256,128]{2,1,0:T(8,128)(2,1)} %copy-done.5, bf16[4,256,1024]{2,1,0:T(8,128)(2,1)} %copy-done.4, bf16[5,32,128]{2,1,0:T(8,128)(2,1)} %pack.1.rest_0_, ...), custom_call_target="tpu_custom_call" | custom-call | flops 44000002048 | tf_op jit(solution)/shard_map/attend/pallas_call | solution.py:281
  132.8 36.8 %all_to_all.10 = bf16[256,16,128]{2,1,0:T(8,128)(2,1)S(1)} all-to-all(bf16[256,16,128]{2,1,0:T(8,128)(2,1)} %bitcast.26), channel_id=1, replica_groups=mesh['dap'=64,'head'=4] {'head','dap'}, dimensions={0} | all-to-all | bytes 2097152 | tf_op jit(solution)/shard_map/all_to_all | solution.py:363
  (83 shorter events, 16.5 us)
Async XLA Ops:
  0.0 12.7 %collective-permute-start = (bf16[1,128]{1,0:T(2,128)(2,1)}, bf16[1,128]{1,0:T(2,128)(2,1)S(1)}, u32[]{:S(2)}, u32[]{:S(2)}) collective-permute-start(bf16[1,128]{1,0:T(2,128)(2,1)} %bitcast.27), channel_id=1, source_target_pairs={{0,2},{1,3},{2,0},{3,1},{4,6},{5,7},{6,4},{7,5},{8,10},{9,11},{10,... | collective-permute-start | bytes 776 | tf_op jit(solution)/shard_map/ppermute | solution.py:348
  14.0 15.6 %collective-permute-start.14 = (bf16[2,16,1024]{2,1,0:T(8,128)(2,1)S(1)}, bf16[2,16,1024]{2,1,0:T(8,128)(2,1)S(1)}, u32[]{:S(2)}, u32[]{:S(2)}) collective-permute-start(bf16[2,16,1024]{2,1,0:T(8,128)(2,1)S(1)} %bias.1), channel_id=1, source_target_pairs={{0,6},{1,7},{2,4},{3,5},{4,2},{5,3},{6,0},{7,1},{8,14},{9,15},{10,... | collective-permute-start | bytes 196616 | tf_op jit(solution)/shard_map/ppermute | solution.py:321
  16.0 9.8 %collective-permute-start.7 = (bf16[2,16,1024]{2,1,0:T(8,128)(2,1)S(1)}, bf16[2,16,1024]{2,1,0:T(8,128)(2,1)S(1)}, u32[]{:S(2)}, u32[]{:S(2)}) collective-permute-start(bf16[2,16,1024]{2,1,0:T(8,128)(2,1)S(1)} %bias.1), channel_id=1, source_target_pairs={{0,62},{1,63},{2,60},{3,61},{4,58},{5,59},{6,56},{7,57},{8,6},{9,7... | collective-permute-start | bytes 196616 | tf_op jit(solution)/shard_map/ppermute | solution.py:321
  22.1 3.7 %collective-permute-start.6 = (bf16[2,16,1024]{2,1,0:T(8,128)(2,1)S(1)}, bf16[2,16,1024]{2,1,0:T(8,128)(2,1)S(1)}, u32[]{:S(2)}, u32[]{:S(2)}) collective-permute-start(bf16[2,16,1024]{2,1,0:T(8,128)(2,1)S(1)} %bias.1), channel_id=1, source_target_pairs={{0,56},{1,57},{2,58},{3,59},{4,60},{5,61},{6,62},{7,63},{8,0},{9,1... | collective-permute-start | bytes 196616 | tf_op jit(solution)/shard_map/ppermute | solution.py:321
  22.8 6.4 %collective-permute-start.2 = (bf16[2,16,1024]{2,1,0:T(8,128)(2,1)S(1)}, bf16[2,16,1024]{2,1,0:T(8,128)(2,1)S(1)}, u32[]{:S(2)}, u32[]{:S(2)}) collective-permute-start(bf16[2,16,1024]{2,1,0:T(8,128)(2,1)S(1)} %bias.1), channel_id=1, source_target_pairs={{0,14},{1,15},{2,12},{3,13},{4,10},{5,11},{6,8},{7,9},{8,22},{9,23... | collective-permute-start | bytes 196616 | tf_op jit(solution)/shard_map/ppermute | solution.py:321
  25.2 4.3 %collective-permute-start.1 = (bf16[2,16,1024]{2,1,0:T(8,128)(2,1)S(1)}, bf16[2,16,1024]{2,1,0:T(8,128)(2,1)S(1)}, u32[]{:S(2)}, u32[]{:S(2)}) collective-permute-start(bf16[2,16,1024]{2,1,0:T(8,128)(2,1)S(1)} %bias.1), channel_id=1, source_target_pairs={{0,8},{1,9},{2,10},{3,11},{4,12},{5,13},{6,14},{7,15},{8,16},{9,17... | collective-permute-start | bytes 196616 | tf_op jit(solution)/shard_map/ppermute | solution.py:321
  25.8 6.9 %collective-permute-start.8 = (bf16[2,32,1024]{2,1,0:T(8,128)(2,1)S(1)}, bf16[2,32,1024]{2,1,0:T(8,128)(2,1)S(1)}, u32[]{:S(2)}, u32[]{:S(2)}) collective-permute-start(bf16[2,32,1024]{2,1,0:T(8,128)(2,1)S(1)} %pad_maximum_fusion.1), channel_id=1, source_target_pairs={{0,56},{1,57},{2,58},{3,59},{4,60},{5,61},{6,62},{7,63},{8,0},{9,1... | collective-permute-start | bytes 393224 | tf_op jit(solution)/shard_map/ppermute | solution.py:321
  29.5 5.9 %collective-permute-start.3 = (bf16[2,32,1024]{2,1,0:T(8,128)(2,1)S(1)}, bf16[2,32,1024]{2,1,0:T(8,128)(2,1)S(1)}, u32[]{:S(2)}, u32[]{:S(2)}) collective-permute-start(bf16[2,32,1024]{2,1,0:T(8,128)(2,1)S(1)} %pad_maximum_fusion), channel_id=1, source_target_pairs={{0,8},{1,9},{2,10},{3,11},{4,12},{5,13},{6,14},{7,15},{8,16},{9,17... | collective-permute-start | bytes 393224 | tf_op jit(solution)/shard_map/ppermute | solution.py:321
  32.7 4.6 %collective-permute-start.9 = (bf16[2,32,1024]{2,1,0:T(8,128)(2,1)S(1)}, bf16[2,32,1024]{2,1,0:T(8,128)(2,1)S(1)}, u32[]{:S(2)}, u32[]{:S(2)}) collective-permute-start(bf16[2,32,1024]{2,1,0:T(8,128)(2,1)S(1)} %collective-permute-done.8), channel_id=1, source_target_pairs={{0,56},{1,57},{2,58},{3,59},{4,60},{5,61},{6,62},{7,63},{8,0},{9,1... | collective-permute-start | bytes 393224 | tf_op jit(solution)/shard_map/ppermute | solution.py:321
  35.4 5.0 %collective-permute-start.4 = (bf16[2,32,1024]{2,1,0:T(8,128)(2,1)S(1)}, bf16[2,32,1024]{2,1,0:T(8,128)(2,1)S(1)}, u32[]{:S(2)}, u32[]{:S(2)}) collective-permute-start(bf16[2,32,1024]{2,1,0:T(8,128)(2,1)S(1)} %collective-permute-done.3), channel_id=1, source_target_pairs={{0,8},{1,9},{2,10},{3,11},{4,12},{5,13},{6,14},{7,15},{8,16},{9,17... | collective-permute-start | bytes 393224 | tf_op jit(solution)/shard_map/ppermute | solution.py:321
  37.4 4.6 %collective-permute-start.10 = (bf16[1,32,1024]{2,1,0:T(8,128)(2,1)S(1)}, bf16[1,32,1024]{2,1,0:T(8,128)(2,1)S(1)}, u32[]{:S(2)}, u32[]{:S(2)}) collective-permute-start(bf16[1,32,1024]{2,1,0:T(8,128)(2,1)S(1)} %slice.17), channel_id=1, source_target_pairs={{0,56},{1,57},{2,58},{3,59},{4,60},{5,61},{6,62},{7,63},{8,0},{9,1... | collective-permute-start | bytes 196616 | tf_op jit(solution)/shard_map/ppermute | solution.py:321
  40.4 5.1 %collective-permute-start.5 = (bf16[1,32,1024]{2,1,0:T(8,128)(2,1)S(1)}, bf16[1,32,1024]{2,1,0:T(8,128)(2,1)S(1)}, u32[]{:S(2)}, u32[]{:S(2)}) collective-permute-start(bf16[1,32,1024]{2,1,0:T(8,128)(2,1)S(1)} %slice.16), channel_id=1, source_target_pairs={{0,8},{1,9},{2,10},{3,11},{4,12},{5,13},{6,14},{7,15},{8,16},{9,17... | collective-permute-start | bytes 196616 | tf_op jit(solution)/shard_map/ppermute | solution.py:321
  46.2 25.2 %collective-permute-start.16 = (bf16[2,256,1024]{2,1,0:T(8,128)(2,1)}, bf16[2,256,1024]{2,1,0:T(8,128)(2,1)S(1)}, u32[]{:S(2)}, u32[]{:S(2)}) collective-permute-start(bf16[2,256,1024]{2,1,0:T(8,128)(2,1)} %maximum_dynamic-update-slice_fusion.rest_4_), channel_id=1, source_target_pairs={{0,64},{1,65},{2,66},{3,67},{4,68},{5,69},{6,70},{7,71},{8,72},{9,... | collective-permute-start | bytes 3145736 | tf_op jit(solution)/shard_map/ppermute | solution.py:321
  47.4 36.4 %collective-permute-start.15 = (bf16[2,256,1024]{2,1,0:T(8,128)(2,1)}, bf16[2,256,1024]{2,1,0:T(8,128)(2,1)S(1)}, u32[]{:S(2)}, u32[]{:S(2)}) collective-permute-start(bf16[2,256,1024]{2,1,0:T(8,128)(2,1)} %maximum_dynamic-update-slice_fusion.rest_4_), channel_id=1, source_target_pairs={{0,192},{1,193},{2,194},{3,195},{4,196},{5,197},{6,198},{7,199},{8... | collective-permute-start | bytes 3145736 | tf_op jit(solution)/shard_map/ppermute | solution.py:321
  48.9 50.7 %all-to-all-start = ((bf16[64,4,16,128]{3,2,1,0:T(8,128)(2,1)}), bf16[64,4,16,128]{3,2,1,0:T(8,128)(2,1)S(1)}, u32[]{:S(2)}, u32[]{:S(2)}) async-start(bf16[64,4,16,128]{3,2,1,0:T(8,128)(2,1)} %bitcast.22), calls=%async_computation | async-start | bytes 2097152 | tf_op jit(solution)/shard_map/all_to_all | solution.py:360
  55.1 28.8 %collective-permute-start.13 = (bf16[5,32,128]{2,1,0:T(8,128)(2,1)}, bf16[5,32,128]{2,1,0:T(8,128)(2,1)S(1)}, u32[]{:S(2)}, u32[]{:S(2)}) collective-permute-start(bf16[5,32,128]{2,1,0:T(8,128)(2,1)} %pack.1.rest_0_), channel_id=1, source_target_pairs={{0,3},{1,2},{2,1},{3,0},{4,7},{5,6},{6,5},{7,4},{8,11},{9,10},{10,... | collective-permute-start | bytes 122888 | tf_op jit(solution)/shard_map/ppermute | solution.py:354
  62.2 24.5 %collective-permute-start.12 = (bf16[5,32,128]{2,1,0:T(8,128)(2,1)}, bf16[5,32,128]{2,1,0:T(8,128)(2,1)S(1)}, u32[]{:S(2)}, u32[]{:S(2)}) collective-permute-start(bf16[5,32,128]{2,1,0:T(8,128)(2,1)} %pack.1.rest_0_), channel_id=1, source_target_pairs={{0,1},{1,0},{2,3},{3,2},{4,5},{5,4},{6,7},{7,6},{8,9},{9,8},{10,11... | collective-permute-start | bytes 122888 | tf_op jit(solution)/shard_map/ppermute | solution.py:354
  62.2 25.1 %collective-permute-start.11 = (bf16[5,32,128]{2,1,0:T(8,128)(2,1)}, bf16[5,32,128]{2,1,0:T(8,128)(2,1)S(1)}, u32[]{:S(2)}, u32[]{:S(2)}) collective-permute-start(bf16[5,32,128]{2,1,0:T(8,128)(2,1)} %pack.1.rest_0_), channel_id=1, source_target_pairs={{0,2},{1,3},{2,0},{3,1},{4,6},{5,7},{6,4},{7,5},{8,10},{9,11},{10,... | collective-permute-start | bytes 122888 | tf_op jit(solution)/shard_map/ppermute | solution.py:354
  71.4 28.1 %collective-permute-start.19 = (bf16[2,256,1024]{2,1,0:T(8,128)(2,1)}, bf16[2,256,1024]{2,1,0:T(8,128)(2,1)}, u32[]{:S(2)}, u32[]{:S(2)}) collective-permute-start(bf16[2,256,1024]{2,1,0:T(8,128)(2,1)} %maximum_dynamic-update-slice_fusion.rest_4_), channel_id=1, source_target_pairs={{0,1},{1,0},{2,3},{3,2},{4,5},{5,4},{6,7},{7,6},{8,9},{9,8},{10,11... | collective-permute-start | bytes 3145736 | tf_op jit(solution)/shard_map/ppermute | solution.py:340
  83.8 14.9 %collective-permute-start.17 = (bf16[1,256,1024]{2,1,0:T(8,128)(2,1)S(1)}, bf16[1,256,1024]{2,1,0:T(8,128)(2,1)}, u32[]{:S(2)}, u32[]{:S(2)}) collective-permute-start(bf16[1,256,1024]{2,1,0:T(8,128)(2,1)S(1)} %slice.18), channel_id=1, source_target_pairs={{0,64},{1,65},{2,66},{3,67},{4,68},{5,69},{6,70},{7,71},{8,72},{9,... | collective-permute-start | bytes 1572872 | tf_op jit(solution)/shard_map/ppermute | solution.py:321
  83.9 15.6 %collective-permute-start.18 = (bf16[1,256,1024]{2,1,0:T(8,128)(2,1)S(1)}, bf16[1,256,1024]{2,1,0:T(8,128)(2,1)}, u32[]{:S(2)}, u32[]{:S(2)}) collective-permute-start(bf16[1,256,1024]{2,1,0:T(8,128)(2,1)S(1)} %slice.19), channel_id=1, source_target_pairs={{0,192},{1,193},{2,194},{3,195},{4,196},{5,197},{6,198},{7,199},{8... | collective-permute-start | bytes 1572872 | tf_op jit(solution)/shard_map/ppermute | solution.py:321
  86.7 14.7 %collective-permute-start.23 = (bf16[2,256,1024]{2,1,0:T(8,128)(2,1)S(1)}, bf16[2,256,1024]{2,1,0:T(8,128)(2,1)}, u32[]{:S(2)}, u32[]{:S(2)}) collective-permute-start(bf16[2,256,1024]{2,1,0:T(8,128)(2,1)S(1)} %collective-permute-done.16.rest_8_), channel_id=1, source_target_pairs={{0,1},{1,0},{2,3},{3,2},{4,5},{5,4},{6,7},{7,6},{8,9},{9,8},{10,11... | collective-permute-start | bytes 3145736 | tf_op jit(solution)/shard_map/ppermute | solution.py:340
  87.2 14.9 %collective-permute-start.20 = (bf16[2,256,1024]{2,1,0:T(8,128)(2,1)S(1)}, bf16[2,256,1024]{2,1,0:T(8,128)(2,1)}, u32[]{:S(2)}, u32[]{:S(2)}) collective-permute-start(bf16[2,256,1024]{2,1,0:T(8,128)(2,1)S(1)} %collective-permute-done.15.rest_5_), channel_id=1, source_target_pairs={{0,1},{1,0},{2,3},{3,2},{4,5},{5,4},{6,7},{7,6},{8,9},{9,8},{10,11... | collective-permute-start | bytes 3145736 | tf_op jit(solution)/shard_map/ppermute | solution.py:340
  98.7 2.7 %collective-permute-start.21 = (bf16[1,256,1024]{2,1,0:T(8,128)(2,1)}, bf16[1,256,1024]{2,1,0:T(8,128)(2,1)}, u32[]{:S(2)}, u32[]{:S(2)}) collective-permute-start(bf16[1,256,1024]{2,1,0:T(8,128)(2,1)} %collective-permute-done.17.rest_6_), channel_id=1, source_target_pairs={{0,1},{1,0},{2,3},{3,2},{4,5},{5,4},{6,7},{7,6},{8,9},{9,8},{10,11... | collective-permute-start | bytes 1572872 | tf_op jit(solution)/shard_map/ppermute | solution.py:340
  (14 other events, 133.4 us)

commit v2 on v1

--- a/solution.py
+++ b/solution.py
@@ -322,10 +322,9 @@
 
 
 def gather_bias(rows, out):
-    beside = send(rows, 0, 0, 1)
-    up = jnp.concatenate([send(rows, 0, 1), send(rows, 0, 1, 1)], 1)
-    down = jnp.concatenate([send(rows, 0, -1), send(rows, 0, -1, 1)], 1)
-    near = jnp.concatenate([rows, beside, up, down], 1)
+    both = jnp.concatenate([rows, send(rows, 0, 0, 1)], 1)
+    up, down = send(both, 0, 1), send(both, 0, -1)
+    near = jnp.concatenate([both, up, down], 1)
     got = []
     for step in range(2, 4):
         up, down = send(up, 0, 1), send(down, 0, -1)

time: 172 us -> 176 us (1.023)
  local copies, waits for them, and re-layouts: 11.9 us -> 16.9 us
  waiting for transfers between devices: 27.9 us -> 25.5 us
    unnamed x36 -> x38, local copies, waits for them, and re-layouts: 8.18 us -> 13.2 us
    ppermute x15 -> x13, starting transfers between devices: 25.3 us -> 22.4 us  [send(): return lax.ppermute(value, ('dap', 'head'), pairs)]
    ppermute x15 -> x13, waiting for transfers between devices: 25.3 us -> 22.9 us  [send(): return lax.ppermute(value, ('dap', 'head'), pairs)]
    ppermute x5, starting transfers between devices: 13.8 us -> 15.8 us  [gather_bias(): return (own + [lax.ppermute(piece, 'head', swap) for piece in own], out)]
  transfers between devices with their start and end apart: 25 -> 23, of which waited for: 9 -> 11; matrix products, arithmetic and copies ran while one was open for 5% -> 4% of each run, Pallas kernels for 5% -> 5%
where the time goes in v2:
time: 176 us; the launch traced here: 175 us
  starting transfers between devices  54.9 us (31%)
  Pallas kernels  40.1 us (23%)
  blocking collectives  37.1 us (21%)
  waiting for transfers between devices  25.5 us (14%)
  local copies, waits for them, and re-layouts  16.9 us (10%)
    all_to_all x1, blocking collectives, body(): update = lax.all_to_all(update, ('head', 'dap'), 0, 0, tiled=True)  37.1 us
    pallas_call x1, Pallas kernels, attend_call(): pl.pallas_call(attend_kernel, grid=(N // TILE,), in_specs=[pl.BlockSpec(m...  30.6 us
    ppermute x13, waiting for transfers between devices, send(): return lax.ppermute(value, ('dap', 'head'), pairs)  22.9 us
    ppermute x13, starting transfers between devices, send(): return lax.ppermute(value, ('dap', 'head'), pairs)  22.4 us
    ppermute x5, starting transfers between devices, gather_bias(): return (own + [lax.ppermute(piece, 'head', swap) for piece in own], out)  15.8 us
    unnamed x38, local copies, waits for them, and re-layouts  13.2 us
    ppermute x3, starting transfers between devices, body(): lax.ppermute(mine, 'head', [(h, h ^ n) for h in range(HEADS)])  8.61 us
    all_to_all x1, starting transfers between devices, body(): recv = lax.all_to_all(out, 'dap', 0, 0, tiled=True)  5.93 us
  transfers between devices with their start and end apart: 23, of which 11 were waited for; matrix products, arithmetic and copies ran while one was open for 4% of the time, Pallas kernels for 5%

profile of v2, /device:TPU:1, one launch (start us, length us, event | category | flops | bytes accessed | tf_op | source)
XLA Modules:
  0.0 175.5 jit_solution(28116213545966833)
XLA Ops:
  0.0 2.1 %collective-permute-start = (bf16[1,128]{1,0:T(2,128)(2,1)}, bf16[1,128]{1,0:T(2,128)(2,1)S(1)}, u32[]{:S(2)}, u32[]{:S(2)}) collective-permute-start(bf16[1,128]{1,0:T(2,128)(2,1)} %bitcast.27), channel_id=1, source_target_pairs={{0,2},{1,3},{2,0},{3,1},{4,6},{5,7},{6,4},{7,5},{8,10},{9,11},{10,... | collective-permute-start | bytes 776 | tf_op jit(solution)/shard_map/ppermute | solution.py:347
  4.0 2.4 %mask.1 = (bf16[4,256,1024]{2,1,0:T(8,128)(2,1)S(1)}, bf16[4,256,128]{2,1,0:T(8,128)(2,1)S(1)}) custom-call(s32[3]{0:T(128)S(1)} %pad_add_fusion.place_ref, s32[1,1024]{1,0:T(1,128)S(1)} %bitcast.23, s32[1,1024]{1,0:T(1,128)S(1)} %bitcast.24), custom_call_target="tpu_custom_call" | custom-call | flops 2200000000 | tf_op jit(solution)/shard_map/mask/pallas_call | solution.py:142
  6.4 1.4 copy-done.6
  8.4 4.5 %norm.1 = (bf16[16,1024,128]{2,1,0:T(8,128)(2,1)S(1)}, bf16[4,16,64,128]{3,2,1,0:T(8,128)(2,1)S(1)}) custom-call(s32[1]{0:T(128)} %bitcast.4.head_ref, bf16[16,1024,128]{2,1,0:T(8,128)(2,1)S(1)} %copy-done.1), custom_call_target="tpu_custom_call" | custom-call | flops 6600000000 | bytes 9437184 | tf_op jit(solution)/shard_map/norm/pallas_call | solution.py:52
  13.0 2.0 %copy-done.4 = bf16[16,1024,128]{2,1,0:T(8,128)(2,1)} copy-done((bf16[16,1024,128]{2,1,0:T(8,128)(2,1)}, bf16[16,1024,128]{2,1,0:T(8,128)(2,1)S(1)}, u32[]{:S(2)}) %copy-start.4) | copy-done | bytes 4194328
  15.1 2.2 %copy-done.5 = bf16[16,1024,128]{2,1,0:T(8,128)(2,1)S(1)} copy-done((bf16[16,1024,128]{2,1,0:T(8,128)(2,1)S(1)}, bf16[16,1024,128]{2,1,0:T(8,128)(2,1)}, u32[]{:S(2)}) %copy-start.5) | copy-done | bytes 4194328
  18.5 2.0 %collective-permute-start.1 = (bf16[2,16,1024]{2,1,0:T(8,128)(2,1)S(1)}, bf16[2,16,1024]{2,1,0:T(8,128)(2,1)S(1)}, u32[]{:S(2)}, u32[]{:S(2)}) collective-permute-start(bf16[2,16,1024]{2,1,0:T(8,128)(2,1)S(1)} %bias.1), channel_id=1, source_target_pairs={{0,6},{1,7},{2,4},{3,5},{4,2},{5,3},{6,0},{7,1},{8,14},{9,15},{10,... | collective-permute-start | bytes 196616 | tf_op jit(solution)/shard_map/ppermute | solution.py:321
  20.5 1.6 copy.22
  22.9 5.7 %collective-permute-start.6 = (bf16[2,32,1024]{2,1,0:T(8,128)(2,1)S(1)}, bf16[2,32,1024]{2,1,0:T(8,128)(2,1)S(1)}, u32[]{:S(2)}, u32[]{:S(2)}) collective-permute-start(bf16[2,32,1024]{2,1,0:T(8,128)(2,1)S(1)} %pad_maximum_fusion), channel_id=1, source_target_pairs={{0,56},{1,57},{2,58},{3,59},{4,60},{5,61},{6,62},{7,63},{8,0},{9,1... | collective-permute-start | bytes 393224 | tf_op jit(solution)/shard_map/ppermute | solution.py:321
  30.5 3.1 %collective-permute-start.7 = (bf16[2,32,1024]{2,1,0:T(8,128)(2,1)S(1)}, bf16[2,32,1024]{2,1,0:T(8,128)(2,1)S(1)}, u32[]{:S(2)}, u32[]{:S(2)}) collective-permute-start(bf16[2,32,1024]{2,1,0:T(8,128)(2,1)S(1)} %collective-permute-done.6), channel_id=1, source_target_pairs={{0,56},{1,57},{2,58},{3,59},{4,60},{5,61},{6,62},{7,63},{8,0},{9,1... | collective-permute-start | bytes 393224 | tf_op jit(solution)/shard_map/ppermute | solution.py:321
  35.6 3.1 %collective-permute-start.8 = (bf16[2,32,1024]{2,1,0:T(8,128)(2,1)S(1)}, bf16[2,32,1024]{2,1,0:T(8,128)(2,1)S(1)}, u32[]{:S(2)}, u32[]{:S(2)}) collective-permute-start(bf16[2,32,1024]{2,1,0:T(8,128)(2,1)S(1)} %collective-permute-done.7), channel_id=1, source_target_pairs={{0,56},{1,57},{2,58},{3,59},{4,60},{5,61},{6,62},{7,63},{8,0},{9,1... | collective-permute-start | bytes 393224 | tf_op jit(solution)/shard_map/ppermute | solution.py:321
  40.7 3.1 %collective-permute-start.9 = (bf16[1,32,1024]{2,1,0:T(8,128)(2,1)S(1)}, bf16[1,32,1024]{2,1,0:T(8,128)(2,1)S(1)}, u32[]{:S(2)}, u32[]{:S(2)}) collective-permute-start(bf16[1,32,1024]{2,1,0:T(8,128)(2,1)S(1)} %slice.17), channel_id=1, source_target_pairs={{0,56},{1,57},{2,58},{3,59},{4,60},{5,61},{6,62},{7,63},{8,0},{9,1... | collective-permute-start | bytes 196616 | tf_op jit(solution)/shard_map/ppermute | solution.py:321
  45.7 3.6 %collective-permute-done.5 = bf16[1,32,1024]{2,1,0:T(8,128)(2,1)S(1)} collective-permute-done((bf16[1,32,1024]{2,1,0:T(8,128)(2,1)S(1)}, bf16[1,32,1024]{2,1,0:T(8,128)(2,1)S(1)}, u32[]{:S(2)}, u32[]{:S(2)}) %collective-permute-start.5) | collective-permute-done | bytes 65568 | tf_op jit(solution)/shard_map/ppermute | solution.py:321
  51.1 1.5 collective-permute-start.13
  52.6 5.9 %all-to-all-start = ((bf16[64,4,16,128]{3,2,1,0:T(8,128)(2,1)}), bf16[64,4,16,128]{3,2,1,0:T(8,128)(2,1)S(1)}, u32[]{:S(2)}, u32[]{:S(2)}) async-start(bf16[64,4,16,128]{3,2,1,0:T(8,128)(2,1)} %bitcast.22), calls=%async_computation | async-start | bytes 2097152 | tf_op jit(solution)/shard_map/all_to_all | solution.py:359
  58.6 1.4 pack.1.rest_0_
  59.9 8.2 %collective-permute-start.12 = (bf16[5,32,128]{2,1,0:T(8,128)(2,1)}, bf16[5,32,128]{2,1,0:T(8,128)(2,1)S(1)}, u32[]{:S(2)}, u32[]{:S(2)}) collective-permute-start(bf16[5,32,128]{2,1,0:T(8,128)(2,1)} %pack.1.rest_0_), channel_id=1, source_target_pairs={{0,3},{1,2},{2,1},{3,0},{4,7},{5,6},{6,5},{7,4},{8,11},{9,10},{10,... | collective-permute-start | bytes 122888 | tf_op jit(solution)/shard_map/ppermute | solution.py:353
  68.6 4.5 %collective-permute-done.14.rest_8_ = bf16[2,256,1024]{2,1,0:T(8,128)(2,1)S(1)} collective-permute-done((bf16[2,256,1024]{2,1,0:T(8,128)(2,1)}, bf16[2,256,1024]{2,1,0:T(8,128)(2,1)S(1)}, u32[]{:S(2)}, u32[]{:S(2)}) %collective-permute-start.14) | collective-permute-done | bytes 1048608 | tf_op jit(solution)/shard_map/ppermute | solution.py:321
  73.1 14.4 %collective-permute-start.17 = (bf16[2,256,1024]{2,1,0:T(8,128)(2,1)}, bf16[2,256,1024]{2,1,0:T(8,128)(2,1)}, u32[]{:S(2)}, u32[]{:S(2)}) collective-permute-start(bf16[2,256,1024]{2,1,0:T(8,128)(2,1)} %maximum_dynamic-update-slice_fusion.rest_4_), channel_id=1, source_target_pairs={{0,1},{1,0},{2,3},{3,2},{4,5},{5,4},{6,7},{7,6},{8,9},{9,8},{10,11... | collective-permute-start | bytes 3145736 | tf_op jit(solution)/shard_map/ppermute | solution.py:339
  87.7 2.7 %collective-permute-start.16 = (bf16[1,256,1024]{2,1,0:T(8,128)(2,1)S(1)}, bf16[1,256,1024]{2,1,0:T(8,128)(2,1)}, u32[]{:S(2)}, u32[]{:S(2)}) collective-permute-start(bf16[1,256,1024]{2,1,0:T(8,128)(2,1)S(1)} %slice.19), channel_id=1, source_target_pairs={{0,192},{1,193},{2,194},{3,195},{4,196},{5,197},{6,198},{7,199},{8... | collective-permute-start | bytes 1572872 | tf_op jit(solution)/shard_map/ppermute | solution.py:321
  91.1 11.4 %collective-permute-done.15.rest_6_ = bf16[1,256,1024]{2,1,0:T(8,128)(2,1)} collective-permute-done((bf16[1,256,1024]{2,1,0:T(8,128)(2,1)S(1)}, bf16[1,256,1024]{2,1,0:T(8,128)(2,1)}, u32[]{:S(2)}, u32[]{:S(2)}) %collective-permute-start.15) | collective-permute-done | bytes 524320 | tf_op jit(solution)/shard_map/ppermute | solution.py:321
  103.3 1.8 %collective-permute-done.19.rest_11_ = bf16[1,256,1024]{2,1,0:T(8,128)(2,1)} collective-permute-done((bf16[1,256,1024]{2,1,0:T(8,128)(2,1)}, bf16[1,256,1024]{2,1,0:T(8,128)(2,1)}, u32[]{:S(2)}, u32[]{:S(2)}) %collective-permute-start.19) | collective-permute-done | bytes 524320 | tf_op jit(solution)/shard_map/ppermute | solution.py:339
  105.9 30.6 %attend.1 = bf16[4,1024,128]{2,1,0:T(8,128)(2,1)} custom-call(s32[3]{0:T(128)} %copy-done, s32[1]{0:T(128)} %bitcast.3.upper_ref, bf16[64,4,16,128]{3,2,1,0:T(8,128)(2,1)} %copy-done.8, bf16[4,256,128]{2,1,0:T(8,128)(2,1)} %copy-done.7, bf16[4,256,1024]{2,1,0:T(8,128)(2,1)} %copy-done.6, bf16[5,32,128]{2,1,0:T(8,128)(2,1)} %pack.1.rest_0_, ...), custom_call_target="tpu_custom_call" | custom-call | flops 44000002048 | tf_op jit(solution)/shard_map/attend/pallas_call | solution.py:281
  136.5 37.1 %all_to_all.10 = bf16[256,16,128]{2,1,0:T(8,128)(2,1)S(1)} all-to-all(bf16[256,16,128]{2,1,0:T(8,128)(2,1)} %bitcast.26), channel_id=1, replica_groups=mesh['dap'=64,'head'=4] {'head','dap'}, dimensions={0} | all-to-all | bytes 2097152 | tf_op jit(solution)/shard_map/all_to_all | solution.py:362
  (80 shorter events, 19.0 us)
Async XLA Ops:
  0.0 15.1 %collective-permute-start = (bf16[1,128]{1,0:T(2,128)(2,1)}, bf16[1,128]{1,0:T(2,128)(2,1)S(1)}, u32[]{:S(2)}, u32[]{:S(2)}) collective-permute-start(bf16[1,128]{1,0:T(2,128)(2,1)} %bitcast.27), channel_id=1, source_target_pairs={{0,2},{1,3},{2,0},{3,1},{4,6},{5,7},{6,4},{7,5},{8,10},{9,11},{10,... | collective-permute-start | bytes 776 | tf_op jit(solution)/shard_map/ppermute | solution.py:347
  18.5 4.4 %collective-permute-start.1 = (bf16[2,16,1024]{2,1,0:T(8,128)(2,1)S(1)}, bf16[2,16,1024]{2,1,0:T(8,128)(2,1)S(1)}, u32[]{:S(2)}, u32[]{:S(2)}) collective-permute-start(bf16[2,16,1024]{2,1,0:T(8,128)(2,1)S(1)} %bias.1), channel_id=1, source_target_pairs={{0,6},{1,7},{2,4},{3,5},{4,2},{5,3},{6,0},{7,1},{8,14},{9,15},{10,... | collective-permute-start | bytes 196616 | tf_op jit(solution)/shard_map/ppermute | solution.py:321
  22.9 7.6 %collective-permute-start.6 = (bf16[2,32,1024]{2,1,0:T(8,128)(2,1)S(1)}, bf16[2,32,1024]{2,1,0:T(8,128)(2,1)S(1)}, u32[]{:S(2)}, u32[]{:S(2)}) collective-permute-start(bf16[2,32,1024]{2,1,0:T(8,128)(2,1)S(1)} %pad_maximum_fusion), channel_id=1, source_target_pairs={{0,56},{1,57},{2,58},{3,59},{4,60},{5,61},{6,62},{7,63},{8,0},{9,1... | collective-permute-start | bytes 393224 | tf_op jit(solution)/shard_map/ppermute | solution.py:321
  28.6 5.0 %collective-permute-start.2 = (bf16[2,32,1024]{2,1,0:T(8,128)(2,1)S(1)}, bf16[2,32,1024]{2,1,0:T(8,128)(2,1)S(1)}, u32[]{:S(2)}, u32[]{:S(2)}) collective-permute-start(bf16[2,32,1024]{2,1,0:T(8,128)(2,1)S(1)} %pad_maximum_fusion), channel_id=1, source_target_pairs={{0,8},{1,9},{2,10},{3,11},{4,12},{5,13},{6,14},{7,15},{8,16},{9,17... | collective-permute-start | bytes 393224 | tf_op jit(solution)/shard_map/ppermute | solution.py:321
  30.5 5.0 %collective-permute-start.7 = (bf16[2,32,1024]{2,1,0:T(8,128)(2,1)S(1)}, bf16[2,32,1024]{2,1,0:T(8,128)(2,1)S(1)}, u32[]{:S(2)}, u32[]{:S(2)}) collective-permute-start(bf16[2,32,1024]{2,1,0:T(8,128)(2,1)S(1)} %collective-permute-done.6), channel_id=1, source_target_pairs={{0,56},{1,57},{2,58},{3,59},{4,60},{5,61},{6,62},{7,63},{8,0},{9,1... | collective-permute-start | bytes 393224 | tf_op jit(solution)/shard_map/ppermute | solution.py:321
  33.6 5.0 %collective-permute-start.3 = (bf16[2,32,1024]{2,1,0:T(8,128)(2,1)S(1)}, bf16[2,32,1024]{2,1,0:T(8,128)(2,1)S(1)}, u32[]{:S(2)}, u32[]{:S(2)}) collective-permute-start(bf16[2,32,1024]{2,1,0:T(8,128)(2,1)S(1)} %collective-permute-done.2), channel_id=1, source_target_pairs={{0,8},{1,9},{2,10},{3,11},{4,12},{5,13},{6,14},{7,15},{8,16},{9,17... | collective-permute-start | bytes 393224 | tf_op jit(solution)/shard_map/ppermute | solution.py:321
  35.6 5.1 %collective-permute-start.8 = (bf16[2,32,1024]{2,1,0:T(8,128)(2,1)S(1)}, bf16[2,32,1024]{2,1,0:T(8,128)(2,1)S(1)}, u32[]{:S(2)}, u32[]{:S(2)}) collective-permute-start(bf16[2,32,1024]{2,1,0:T(8,128)(2,1)S(1)} %collective-permute-done.7), channel_id=1, source_target_pairs={{0,56},{1,57},{2,58},{3,59},{4,60},{5,61},{6,62},{7,63},{8,0},{9,1... | collective-permute-start | bytes 393224 | tf_op jit(solution)/shard_map/ppermute | solution.py:321
  38.7 5.4 %collective-permute-start.4 = (bf16[2,32,1024]{2,1,0:T(8,128)(2,1)S(1)}, bf16[2,32,1024]{2,1,0:T(8,128)(2,1)S(1)}, u32[]{:S(2)}, u32[]{:S(2)}) collective-permute-start(bf16[2,32,1024]{2,1,0:T(8,128)(2,1)S(1)} %collective-permute-done.3), channel_id=1, source_target_pairs={{0,8},{1,9},{2,10},{3,11},{4,12},{5,13},{6,14},{7,15},{8,16},{9,17... | collective-permute-start | bytes 393224 | tf_op jit(solution)/shard_map/ppermute | solution.py:321
  40.7 5.0 %collective-permute-start.9 = (bf16[1,32,1024]{2,1,0:T(8,128)(2,1)S(1)}, bf16[1,32,1024]{2,1,0:T(8,128)(2,1)S(1)}, u32[]{:S(2)}, u32[]{:S(2)}) collective-permute-start(bf16[1,32,1024]{2,1,0:T(8,128)(2,1)S(1)} %slice.17), channel_id=1, source_target_pairs={{0,56},{1,57},{2,58},{3,59},{4,60},{5,61},{6,62},{7,63},{8,0},{9,1... | collective-permute-start | bytes 196616 | tf_op jit(solution)/shard_map/ppermute | solution.py:321
  44.1 5.2 %collective-permute-start.5 = (bf16[1,32,1024]{2,1,0:T(8,128)(2,1)S(1)}, bf16[1,32,1024]{2,1,0:T(8,128)(2,1)S(1)}, u32[]{:S(2)}, u32[]{:S(2)}) collective-permute-start(bf16[1,32,1024]{2,1,0:T(8,128)(2,1)S(1)} %slice.16), channel_id=1, source_target_pairs={{0,8},{1,9},{2,10},{3,11},{4,12},{5,13},{6,14},{7,15},{8,16},{9,17... | collective-permute-start | bytes 196616 | tf_op jit(solution)/shard_map/ppermute | solution.py:321
  49.9 23.1 %collective-permute-start.14 = (bf16[2,256,1024]{2,1,0:T(8,128)(2,1)}, bf16[2,256,1024]{2,1,0:T(8,128)(2,1)S(1)}, u32[]{:S(2)}, u32[]{:S(2)}) collective-permute-start(bf16[2,256,1024]{2,1,0:T(8,128)(2,1)} %maximum_dynamic-update-slice_fusion.rest_4_), channel_id=1, source_target_pairs={{0,64},{1,65},{2,66},{3,67},{4,68},{5,69},{6,70},{7,71},{8,72},{9,... | collective-permute-start | bytes 3145736 | tf_op jit(solution)/shard_map/ppermute | solution.py:321
  51.1 36.4 %collective-permute-start.13 = (bf16[2,256,1024]{2,1,0:T(8,128)(2,1)}, bf16[2,256,1024]{2,1,0:T(8,128)(2,1)S(1)}, u32[]{:S(2)}, u32[]{:S(2)}) collective-permute-start(bf16[2,256,1024]{2,1,0:T(8,128)(2,1)} %maximum_dynamic-update-slice_fusion.rest_4_), channel_id=1, source_target_pairs={{0,192},{1,193},{2,194},{3,195},{4,196},{5,197},{6,198},{7,199},{8... | collective-permute-start | bytes 3145736 | tf_op jit(solution)/shard_map/ppermute | solution.py:321
  52.6 50.7 %all-to-all-start = ((bf16[64,4,16,128]{3,2,1,0:T(8,128)(2,1)}), bf16[64,4,16,128]{3,2,1,0:T(8,128)(2,1)S(1)}, u32[]{:S(2)}, u32[]{:S(2)}) async-start(bf16[64,4,16,128]{3,2,1,0:T(8,128)(2,1)} %bitcast.22), calls=%async_computation | async-start | bytes 2097152 | tf_op jit(solution)/shard_map/all_to_all | solution.py:359
  59.9 27.7 %collective-permute-start.12 = (bf16[5,32,128]{2,1,0:T(8,128)(2,1)}, bf16[5,32,128]{2,1,0:T(8,128)(2,1)S(1)}, u32[]{:S(2)}, u32[]{:S(2)}) collective-permute-start(bf16[5,32,128]{2,1,0:T(8,128)(2,1)} %pack.1.rest_0_), channel_id=1, source_target_pairs={{0,3},{1,2},{2,1},{3,0},{4,7},{5,6},{6,5},{7,4},{8,11},{9,10},{10,... | collective-permute-start | bytes 122888 | tf_op jit(solution)/shard_map/ppermute | solution.py:353
  68.1 22.3 %collective-permute-start.11 = (bf16[5,32,128]{2,1,0:T(8,128)(2,1)}, bf16[5,32,128]{2,1,0:T(8,128)(2,1)S(1)}, u32[]{:S(2)}, u32[]{:S(2)}) collective-permute-start(bf16[5,32,128]{2,1,0:T(8,128)(2,1)} %pack.1.rest_0_), channel_id=1, source_target_pairs={{0,1},{1,0},{2,3},{3,2},{4,5},{5,4},{6,7},{7,6},{8,9},{9,8},{10,11... | collective-permute-start | bytes 122888 | tf_op jit(solution)/shard_map/ppermute | solution.py:353
  68.2 22.8 %collective-permute-start.10 = (bf16[5,32,128]{2,1,0:T(8,128)(2,1)}, bf16[5,32,128]{2,1,0:T(8,128)(2,1)S(1)}, u32[]{:S(2)}, u32[]{:S(2)}) collective-permute-start(bf16[5,32,128]{2,1,0:T(8,128)(2,1)} %pack.1.rest_0_), channel_id=1, source_target_pairs={{0,2},{1,3},{2,0},{3,1},{4,6},{5,7},{6,4},{7,5},{8,10},{9,11},{10,... | collective-permute-start | bytes 122888 | tf_op jit(solution)/shard_map/ppermute | solution.py:353
  73.1 32.8 %copy-start.9 = (bf16[2,256,1024]{2,1,0:T(8,128)(2,1)}, bf16[2,256,1024]{2,1,0:T(8,128)(2,1)S(1)}, u32[]{:S(2)}) copy-start(bf16[2,256,1024]{2,1,0:T(8,128)(2,1)S(1)} %collective-permute-done.14.rest_8_) | copy-start | bytes 3145732
  73.1 30.2 %collective-permute-start.17 = (bf16[2,256,1024]{2,1,0:T(8,128)(2,1)}, bf16[2,256,1024]{2,1,0:T(8,128)(2,1)}, u32[]{:S(2)}, u32[]{:S(2)}) collective-permute-start(bf16[2,256,1024]{2,1,0:T(8,128)(2,1)} %maximum_dynamic-update-slice_fusion.rest_4_), channel_id=1, source_target_pairs={{0,1},{1,0},{2,3},{3,2},{4,5},{5,4},{6,7},{7,6},{8,9},{9,8},{10,11... | collective-permute-start | bytes 3145736 | tf_op jit(solution)/shard_map/ppermute | solution.py:339
  87.5 14.9 %collective-permute-start.15 = (bf16[1,256,1024]{2,1,0:T(8,128)(2,1)S(1)}, bf16[1,256,1024]{2,1,0:T(8,128)(2,1)}, u32[]{:S(2)}, u32[]{:S(2)}) collective-permute-start(bf16[1,256,1024]{2,1,0:T(8,128)(2,1)S(1)} %slice.18), channel_id=1, source_target_pairs={{0,64},{1,65},{2,66},{3,67},{4,68},{5,69},{6,70},{7,71},{8,72},{9,... | collective-permute-start | bytes 1572872 | tf_op jit(solution)/shard_map/ppermute | solution.py:321
  87.7 15.6 %collective-permute-start.16 = (bf16[1,256,1024]{2,1,0:T(8,128)(2,1)S(1)}, bf16[1,256,1024]{2,1,0:T(8,128)(2,1)}, u32[]{:S(2)}, u32[]{:S(2)}) collective-permute-start(bf16[1,256,1024]{2,1,0:T(8,128)(2,1)S(1)} %slice.19), channel_id=1, source_target_pairs={{0,192},{1,193},{2,194},{3,195},{4,196},{5,197},{6,198},{7,199},{8... | collective-permute-start | bytes 1572872 | tf_op jit(solution)/shard_map/ppermute | solution.py:321
  90.4 14.7 %collective-permute-start.21 = (bf16[2,256,1024]{2,1,0:T(8,128)(2,1)S(1)}, bf16[2,256,1024]{2,1,0:T(8,128)(2,1)}, u32[]{:S(2)}, u32[]{:S(2)}) collective-permute-start(bf16[2,256,1024]{2,1,0:T(8,128)(2,1)S(1)} %collective-permute-done.14.rest_8_), channel_id=1, source_target_pairs={{0,1},{1,0},{2,3},{3,2},{4,5},{5,4},{6,7},{7,6},{8,9},{9,8},{10,11... | collective-permute-start | bytes 3145736 | tf_op jit(solution)/shard_map/ppermute | solution.py:339
  91.0 14.9 %collective-permute-start.18 = (bf16[2,256,1024]{2,1,0:T(8,128)(2,1)S(1)}, bf16[2,256,1024]{2,1,0:T(8,128)(2,1)}, u32[]{:S(2)}, u32[]{:S(2)}) collective-permute-start(bf16[2,256,1024]{2,1,0:T(8,128)(2,1)S(1)} %collective-permute-done.13.rest_5_), channel_id=1, source_target_pairs={{0,1},{1,0},{2,3},{3,2},{4,5},{5,4},{6,7},{7,6},{8,9},{9,8},{10,11... | collective-permute-start | bytes 3145736 | tf_op jit(solution)/shard_map/ppermute | solution.py:339
  102.5 2.7 %collective-permute-start.19 = (bf16[1,256,1024]{2,1,0:T(8,128)(2,1)}, bf16[1,256,1024]{2,1,0:T(8,128)(2,1)}, u32[]{:S(2)}, u32[]{:S(2)}) collective-permute-start(bf16[1,256,1024]{2,1,0:T(8,128)(2,1)} %collective-permute-done.15.rest_6_), channel_id=1, source_target_pairs={{0,1},{1,0},{2,3},{3,2},{4,5},{5,4},{6,7},{7,6},{8,9},{9,8},{10,11... | collective-permute-start | bytes 1572872 | tf_op jit(solution)/shard_map/ppermute | solution.py:339
  103.3 2.6 %collective-permute-start.20 = (bf16[1,256,1024]{2,1,0:T(8,128)(2,1)}, bf16[1,256,1024]{2,1,0:T(8,128)(2,1)}, u32[]{:S(2)}, u32[]{:S(2)}) collective-permute-start(bf16[1,256,1024]{2,1,0:T(8,128)(2,1)} %collective-permute-done.16.rest_7_), channel_id=1, source_target_pairs={{0,1},{1,0},{2,3},{3,2},{4,5},{5,4},{6,7},{7,6},{8,9},{9,8},{10,11... | collective-permute-start | bytes 1572872 | tf_op jit(solution)/shard_map/ppermute | solution.py:339
  (14 other events, 101.3 us)
